TPU v7x, 512 devices: a whole 4x8x8 slice. The times are simulated.
512 devices in a mesh: dp: 32 (over x_lo, y, core), block: 16 (over z, x_hi).
Axes of the slice: x: 4 (x_hi: 2, x_lo: 2; x = x_hi * 2 + x_lo), y: 8, z: 8, core: 2. Of those that a mesh axis runs over, the one named last changes fastest.
Arguments:
- act_rows: bfloat16 [2, 4, 512, 5120], P(None, None, 'dp', 'block'), may hold values from -6 to 6
- grad_rows: bfloat16 [2, 4, 512, 5120], P(None, None, 'dp', 'block'), may hold values from -6 to 6
- eig_act: bfloat16 [2, 16, 320, 320], P(None, 'block'), may hold values from -0.3125 to 0.3125
- eig_grad: bfloat16 [2, 16, 320, 320], P(None, 'block'), may hold values from -0.3125 to 0.3125
- precond: bfloat16 [2, 5120, 10240], P(None, 'block', 'dp'), may hold values from -0.0008544922 to 0.0008544922
- lengths: int32 [4], replicated, may hold values from 128 to 512
Outputs:
- token_influence: float32 [2, 4, 512], P(None, None, ('dp', 'block'))
All inputs are finite; a program needn't handle non-finite values.
Results may differ from a plain program's by a relative error of at most 0.007.
Values may be sent and summed in bfloat16 or wider, within the bound.
No kernel may reach another device: no remote copies, remote signals or barrier semaphores. Data moves between devices by JAX's collectives and lax.ppermute only.
A program may use at most 64 MiB of HBM per device.

v0:
```python
import jax
import jax.numpy as jnp
from jax import lax
from jax.sharding import PartitionSpec as P


def rotate(rows, basis):
    layer_count, seq_count, seq_span, width_all = rows.shape
    block_count, block_size = (basis.shape[1], basis.shape[2])
    blocked = rows.reshape(layer_count, seq_count * seq_span, block_count, block_size)
    turned = jnp.einsum("ltnr,lnrc->ltnc", blocked, basis, preferred_element_type=jnp.float32)
    return turned.astype(jnp.bfloat16).reshape(rows.shape)


def spread(rows, owner_count):
    layer_count = rows.shape[0]
    widened = jnp.broadcast_to(rows[:, None], (layer_count, owner_count) + rows.shape[1:])
    return widened.reshape((layer_count * owner_count,) + rows.shape[1:])


def per_device(act_rows, grad_rows, eig_act, eig_grad, precond, lengths):
    layer_count, seq_count, seq_span, width_local = act_rows.shape
    dp_count = lax.axis_size("dp")
    owner_count = dp_count // layer_count
    act_rot = rotate(act_rows, eig_act)
    grad_rot = rotate(grad_rows, eig_grad)
    gathered = lax.all_gather(act_rot, "block", axis=3, tiled=True)
    range_width = gathered.shape[3] // owner_count
    parted = gathered.reshape(layer_count, seq_count, seq_span, owner_count, range_width)
    act_send = jnp.transpose(parted, (0, 3, 1, 2, 4)).reshape(
        dp_count, seq_count, seq_span, range_width
    )
    grad_send = spread(grad_rot, owner_count)
    act_own, grad_own = (
        lax.all_to_all(act_send, "dp", split_axis=0, concat_axis=2, tiled=True),
        lax.all_to_all(grad_send, "dp", split_axis=0, concat_axis=2, tiled=True),
    )
    tokens = seq_count * act_own.shape[2]
    act_flat = act_own.reshape(tokens, act_own.shape[3])
    grad_flat = grad_own.reshape(tokens, grad_own.shape[3])
    query_count, rows_here, cols_here = precond.shape
    query_table = precond.reshape(query_count * rows_here, cols_here)
    projected = lax.dot_general(
        act_flat, query_table, (((1,), (1,)), ((), ())), preferred_element_type=jnp.float32
    )
    projected = projected.reshape(tokens, query_count, rows_here)
    partial_scores = jnp.einsum(
        "tqr,tr->qt", projected, grad_flat, preferred_element_type=jnp.float32
    )
    partial_scores = partial_scores.reshape(query_count, seq_count, act_own.shape[2])
    summed = lax.psum_scatter(partial_scores, ("dp", "block"), scatter_dimension=2, tiled=True)
    piece_len = summed.shape[2]
    start_pos = lax.axis_index(("dp", "block")) * piece_len
    position = start_pos + jnp.arange(piece_len, dtype=jnp.int32)
    valid_mask = position[None, :] < lengths[:, None]
    return jnp.where(valid_mask[None], summed, 0.0)


def solution(mesh):
    return jax.shard_map(
        per_device,
        mesh=mesh,
        in_specs=(
            P(None, None, "dp", "block"),
            P(None, None, "dp", "block"),
            P(None, "block", None, None),
            P(None, "block", None, None),
            P(None, "block", "dp"),
            P(),
        ),
        out_specs=P(None, None, ("dp", "block")),
        check_vma=False,
    )
```

profile of v0, /device:TPU:1, one launch (start us, length us, event | category | flops | bytes accessed | tf_op | source)
XLA Modules:
  0.0 364.4 jit_solution(16409495259301552751)
XLA Ops:
  6.5 0.0 copy-start
  6.5 1.0 copy-done
  7.6 1.1 convolution_convert_fusion.1
  8.7 1.5 broadcast_in_dim.23
  10.1 0.0 copy-start.2
  10.1 0.0 copy-start.3
  10.1 10.6 %all-to-all-start = ((bf16[32,4,16,320]{3,2,1,0:T(8,128)(2,1)}), bf16[32,4,16,320]{3,2,1,0:T(8,128)(2,1)S(1)}, u32[]{:S(2)}, u32[]{:S(2)}) async-start(bf16[32,4,16,320]{3,2,1,0:T(8,128)(2,1)} %bitcast.45), calls=%async_computation | async-start | bytes 3145728 | tf_op jit(solution)/shard_map/all_to_all | solution.py:36
  20.8 0.0 all-gather.2.cloned.1.call-start
  20.8 0.0 copy-done.2
  20.8 0.0 copy-done.3
  20.9 0.2 convolution_convert_fusion
  21.1 1.2 copy.16
  22.3 0.0 all-gather.2.cloned.1.call-update
  22.3 174.0 %all-gather.2.cloned.1.call-done = bf16[2,4,16,5120]{2,1,0,3:T(4,128)(2,1)} async-done(((bf16[2,4,16,320]{2,1,0,3:T(4,128)(2,1)}), bf16[2,4,16,5120]{2,1,0,3:T(4,128)(2,1)}) %all-gather.2.cloned.1.call-update) | async-done | bytes 1310736 | tf_op jit(solution)/shard_map/all_gather | solution.py:27
  196.3 12.8 %copy.31 = bf16[2,4,16,16,320]{4,2,1,3,0:T(8,128)(2,1)} copy(bf16[2,4,16,16,320]{2,1,0,4,3:T(4,128)(2,1)} %bitcast.43) | data formatting | bytes 2621440 | tf_op jit(solution)/shard_map/transpose | solution.py:30
  209.1 0.0 all-to-all-done
  209.1 0.0 copy-start.4
  209.1 8.2 %all-to-all-start.1 = ((bf16[32,4,16,320]{3,2,1,0:T(8,128)(2,1)}), bf16[32,4,16,320]{3,2,1,0:T(8,128)(2,1)}, u32[]{:S(2)}, u32[]{:S(2)}) async-start(bf16[32,4,16,320]{3,2,1,0:T(8,128)(2,1)} %bitcast.47), calls=%async_computation.1 | async-start | bytes 3145728 | tf_op jit(solution)/shard_map/all_to_all | solution.py:35
  217.2 0.0 copy-done.4
  217.3 0.2 copy.15
  217.4 2.0 bitcast_convert_fusion
  219.4 2.3 copy.33
  221.8 33.8 %all-to-all-done.1 = bf16[32,4,16,320]{3,2,1,0:T(8,128)(2,1)} async-done(((bf16[32,4,16,320]{3,2,1,0:T(8,128)(2,1)}), bf16[32,4,16,320]{3,2,1,0:T(8,128)(2,1)}, u32[]{:S(2)}, u32[]{:S(2)}) %all-to-all-start.1) | async-done | bytes 1310752 | tf_op jit(solution)/shard_map/all_to_all | solution.py:35
  255.6 0.0 copy-start.1
  255.6 1.6 copy.19
  257.2 0.0 copy-done.1
  257.2 1.6 multiply_reduce_fusion
  258.9 0.3 copy.21
  259.2 97.8 %all-reduce = f32[2,4,512]{1,0,2:T(2,128)S(1)} all-reduce(f32[2,4,512]{1,0,2:T(2,128)S(1)} %copy.21), channel_id=2, replica_groups=mesh['dp'=32,'block'=16] {'dp','block'}, use_global_device_ids=true, to_apply=%region_0.0.clone | all-reduce | flops 4096 | bytes 32768
  357.0 0.6 dynamic-slice_select_fusion
  (2 shorter events, 0.0 us)
Async XLA Ops:
  6.5 1.0 copy-start
  10.1 10.7 %copy-start.2 = (bf16[2,1,320,320]{3,2,1,0:T(8,128)(2,1)S(1)}, bf16[2,1,320,320]{3,2,1,0:T(8,128)(2,1)}, u32[]{:S(2)}) copy-start(bf16[2,1,320,320]{3,2,1,0:T(8,128)(2,1)} %param.8) | copy-start | bytes 1228804
  10.1 10.7 %copy-start.3 = (bf16[2,4,16,320]{3,2,1,0:T(8,128)(2,1)S(1)}, bf16[2,4,16,320]{3,2,1,0:T(8,128)(2,1)}, u32[]{:S(2)}) copy-start(bf16[2,4,16,320]{3,2,1,0:T(8,128)(2,1)} %param.6) | copy-start | bytes 245764
  10.1 198.9 %all-to-all-start = ((bf16[32,4,16,320]{3,2,1,0:T(8,128)(2,1)}), bf16[32,4,16,320]{3,2,1,0:T(8,128)(2,1)S(1)}, u32[]{:S(2)}, u32[]{:S(2)}) async-start(bf16[32,4,16,320]{3,2,1,0:T(8,128)(2,1)} %bitcast.45), calls=%async_computation | async-start | bytes 3145728 | tf_op jit(solution)/shard_map/all_to_all | solution.py:36
  20.8 175.5 %all-gather.2.cloned.1.call-start = ((), (), s32[]{:S(2)}) async-start(), calls=%async_computation.2 | async-start | bytes 11141120 | tf_op jit(solution)/shard_map/all_gather | solution.py:27
  209.1 8.2 %copy-start.4 = (s32[4]{0:T(128)S(1)}, s32[4]{0:T(128)}, u32[]{:S(2)}) copy-start(s32[4]{0:T(128)} %param.11) | copy-start | bytes 52
  209.1 46.5 %all-to-all-start.1 = ((bf16[32,4,16,320]{3,2,1,0:T(8,128)(2,1)}), bf16[32,4,16,320]{3,2,1,0:T(8,128)(2,1)}, u32[]{:S(2)}, u32[]{:S(2)}) async-start(bf16[32,4,16,320]{3,2,1,0:T(8,128)(2,1)} %bitcast.47), calls=%async_computation.1 | async-start | bytes 3145728 | tf_op jit(solution)/shard_map/all_to_all | solution.py:35
  255.6 1.6 copy-start.1
Sparse Core Ops, SparseCore 0:
  24.8 171.4 all-gather.1
where the time goes:
time: 365 us; the launch traced here: 364 us
  waiting for transfers between devices  208 us (57%)
  blocking collectives  97.8 us (27%)
  local copies, waits for them, and re-layouts  20.9 us (6%)
  starting transfers between devices  18.8 us (5%)
  between operations  13.5 us (4%)
    all_gather x1, waiting for transfers between devices, per_device(): gathered = lax.all_gather(act_rot, 'block', axis=3, tiled=True)  174 us
    unnamed x1, blocking collectives  97.8 us
    all_to_all x1, waiting for transfers between devices, per_device(): lax.all_to_all(act_send, 'dp', split_axis=0, concat_axis=2, tiled=True)  33.8 us
    transpose x1, local copies, waits for them, and re-layouts, per_device(): jnp.transpose(parted, (0, 3, 1, 2, 4))  12.8 us
    all_to_all x1, starting transfers between devices, per_device(): lax.all_to_all(grad_send, 'dp', split_axis=0, concat_axis=2, tiled=True)  10.6 us
    all_to_all x1, starting transfers between devices, per_device(): lax.all_to_all(act_send, 'dp', split_axis=0, concat_axis=2, tiled=True)  8.16 us
  transfers between devices with their start and end apart: 3, of which 2 were waited for; matrix products, arithmetic and copies ran while one was open for 5% of the time, Pallas kernels for 0%

commit v1 on v0

v1 whole, which is shorter than its diff:
```python
import functools

import jax
import jax.numpy as jnp
from jax import lax
from jax.experimental import pallas as pl
from jax.experimental.pallas import tpu as pltpu
from jax.sharding import Mesh, PartitionSpec as P

AXES = ("xl", "y", "c", "z", "xh")
SIZES = (2, 8, 2, 8, 2)
NT = (((1,), (1,)), ((), ()))


def transposed_plane():
    xl_n, y_n, c_n, z_n, xh_n = SIZES

    def flat(xl, y, c, z, xh):
        return (((xl * y_n + y) * c_n + c) * z_n + z) * xh_n + xh

    return [
        (flat(xl, y, c, z, xh), flat(xl, z, c, y, xh))
        for xl in range(xl_n)
        for y in range(y_n)
        for c in range(c_n)
        for z in range(z_n)
        for xh in range(xh_n)
    ]


def rotate_kernel(rows_ref, basis_ref, out_ref):
    layers, tokens, _ = rows_ref.shape
    half = tokens // 2
    to = lax.broadcasted_iota(jnp.int32, (tokens, tokens), 0)
    came = lax.broadcasted_iota(jnp.int32, (tokens, tokens), 1)
    wanted = jnp.where(to < half, 2 * to, 2 * (to - half) + 1)
    pick = (came == wanted).astype(jnp.bfloat16)
    for layer in range(layers):
        rows = jnp.dot(pick, rows_ref[layer], preferred_element_type=jnp.float32)
        turned = jnp.dot(
            rows.astype(jnp.bfloat16), basis_ref[layer], preferred_element_type=jnp.float32
        ).astype(jnp.bfloat16)
        for copy in range(out_ref.shape[1]):
            for parity in range(2):
                out_ref[layer, copy, parity] = turned[parity * half:(parity + 1) * half]


def rotate(rows, basis, copies):
    layers, seqs, span, width = rows.shape
    tokens = seqs * span
    return pl.pallas_call(
        rotate_kernel,
        out_shape=jax.ShapeDtypeStruct((layers, copies, 2, tokens // 2, width), jnp.bfloat16),
        cost_estimate=pl.CostEstimate(
            flops=2 * layers * tokens * width * width, bytes_accessed=2 << 20, transcendentals=0
        ),
    )(rows.reshape(layers, tokens, width), basis.reshape(layers, width, width))


def score_kernel(act_ref, grad_ref, table_ref, out_ref):
    owners, blocks, tokens, width = act_ref.shape
    queries = table_ref.shape[2]
    total = owners * tokens
    seqs = tokens // 8
    acts = [act_ref[:, block].reshape(total, width) for block in range(blocks)]
    lane = lax.broadcasted_iota(jnp.int32, (owners, 8, 128), 2)
    out = jnp.zeros((owners, 8, 128), jnp.float32)
    for query in range(queries):
        running = jnp.zeros((total, width), jnp.float32)
        for row_block in range(blocks):
            projected = jnp.zeros((total, width), jnp.float32)
            for block in range(blocks):
                projected += lax.dot_general(
                    acts[block], table_ref[block, row_block, query], NT,
                    preferred_element_type=jnp.float32,
                )
            running += projected * grad_ref[:, row_block].reshape(total, width).astype(jnp.float32)
        column = jnp.sum(running, axis=1, keepdims=True).reshape(owners, seqs, 8, 1)
        for seq in range(seqs):
            out = jnp.where(lane == query * seqs + seq, column[:, seq], out)
    out_ref[...] = out


def score(act, grad, table):
    owners, blocks, tokens, width = act.shape
    queries = table.shape[2]
    return pl.pallas_call(
        score_kernel,
        out_shape=jax.ShapeDtypeStruct((owners, 8, 128), jnp.float32),
        cost_estimate=pl.CostEstimate(
            flops=2 * owners * tokens * queries * (blocks * width) ** 2,
            bytes_accessed=4 << 20,
            transcendentals=0,
        ),
        compiler_params=pltpu.CompilerParams(vmem_limit_bytes=40 << 20),
    )(act, grad, table)


def per_device(act_rows, grad_rows, eig_act, eig_grad, precond, lengths):
    xl_n, y_n, c_n, z_n, xh_n = SIZES
    layers, seqs, span, width = act_rows.shape
    tokens = seqs * span // 2
    table = lax.all_gather(precond, ("c", "xh"), axis=0, tiled=False)
    table = table.reshape((c_n, xh_n) + precond.shape)

    act = rotate(act_rows, eig_act, 1)
    act = lax.ppermute(act, AXES, transposed_plane())
    grad = rotate(grad_rows, eig_grad, y_n)
    grad = lax.all_to_all(
        grad.reshape(xl_n * y_n * xh_n, tokens, width), ("xl", "y", "xh"), 0, 0, tiled=True
    )
    act = jnp.broadcast_to(act, (layers, z_n, 2, tokens, width))
    act = lax.all_to_all(
        act.reshape(xl_n * z_n * xh_n, tokens, width), ("xl", "z", "xh"), 0, 0, tiled=True
    )
    partial_scores = score(
        act.reshape(xl_n * y_n, 2, tokens, width), grad.reshape(xl_n * y_n, 2, tokens, width), table
    )
    shares = lax.all_to_all(
        partial_scores.reshape(xl_n * y_n * z_n, 1, 128), ("xl", "y", "z"), 0, 0, tiled=True
    )
    queries = precond.shape[0]
    summed = jnp.sum(shares, axis=(0, 1))[: queries * seqs].reshape(queries, seqs, 1)
    position = lax.axis_index(("xl", "y", "c", "z", "xh"))
    valid_mask = position < lengths
    return jnp.where(valid_mask[None, :, None], summed, 0.0)


def solution(mesh):
    fine = Mesh(mesh.devices.reshape(SIZES), AXES)
    dp, block = ("xl", "y", "c"), ("z", "xh")
    return jax.shard_map(
        per_device,
        mesh=fine,
        in_specs=(
            P(None, None, dp, block),
            P(None, None, dp, block),
            P(None, block, None, None),
            P(None, block, None, None),
            P(None, block, dp),
            P(),
        ),
        out_specs=P(None, None, dp + block),
        check_vma=False,
    )
```

time: 365 us -> 118 us (0.32)
  the two profiles are of different devices: /device:TPU:1 before, /device:TPU:8 now
where the time goes in v1:
time: 118 us; the launch traced here: 117 us
  waiting for transfers between devices  48.1 us (41%)
  starting transfers between devices  44.9 us (38%)
  between operations  13.5 us (11%)
  Pallas kernels  7.55 us (6%)
  local copies, waits for them, and re-layouts  2.65 us (2%)
    all_to_all x1, waiting for transfers between devices, per_device(): lax.all_to_all(act.reshape(xl_n * z_n * xh_n, tokens, width), ('xl', 'z',...  17.8 us
    ppermute x1, waiting for transfers between devices, per_device(): act = lax.ppermute(act, AXES, transposed_plane())  17.2 us
    all_to_all x1, starting transfers between devices, per_device(): lax.all_to_all(act.reshape(xl_n * z_n * xh_n, tokens, width), ('xl', 'z',...  16.6 us
    all_to_all x1, starting transfers between devices, per_device(): lax.all_to_all(partial_scores.reshape(xl_n * y_n * z_n, 1, 128), ('xl', '...  14.2 us
    all_to_all x1, waiting for transfers between devices, per_device(): lax.all_to_all(partial_scores.reshape(xl_n * y_n * z_n, 1, 128), ('xl', '...  12.4 us
    all_to_all x1, starting transfers between devices, per_device(): lax.all_to_all(grad.reshape(xl_n * y_n * xh_n, tokens, width), ('xl', 'y'...  10.2 us
    pallas_call x2, Pallas kernels, rotate(): pl.pallas_call(rotate_kernel, out_shape=jax.ShapeDtypeStruct((layers, cop...  4.66 us
    ppermute x1, starting transfers between devices, per_device(): act = lax.ppermute(act, AXES, transposed_plane())  3.94 us
  transfers between devices with their start and end apart: 5, of which 3 were waited for; matrix products, arithmetic and copies ran while one was open for 1% of the time, Pallas kernels for 2%

profile of v1, /device:TPU:8, one launch (start us, length us, event | category | flops | bytes accessed | tf_op | source)
XLA Modules:
  0.0 117.4 jit_solution(13232562401106207352)
XLA Ops:
  6.5 2.5 %shard_map.65 = bf16[2,8,2,32,320]{4,3,2,1,0:T(8,128)(2,1)} custom-call(bf16[2,64,320]{2,1,0:T(8,128)(2,1)} %bitcast.23, bf16[2,320,320]{2,1,0:T(8,128)(2,1)} %bitcast.20), custom_call_target="tpu_custom_call" | custom-call | flops 26214400 | bytes 2097152 | tf_op jit(solution)/shard_map/pallas_call | solution.py:51
  9.0 10.2 %all-to-all-start.1 = ((bf16[32,32,320]{2,1,0:T(8,128)(2,1)}), bf16[32,32,320]{2,1,0:T(8,128)(2,1)S(1)}, u32[]{:S(2)}, u32[]{:S(2)}) async-start(bf16[32,32,320]{2,1,0:T(8,128)(2,1)} %bitcast.18), calls=%async_computation.1 | async-start | bytes 1572864 | tf_op jit(solution)/shard_map/all_to_all | solution.py:109
  19.2 0.0 all-gather.3.cloned.1.call-start
  19.2 0.7 all-gather.3.cloned.1.call-update
  19.9 2.2 %shard_map.64 = bf16[2,1,2,32,320]{4,3,2,1,0:T(8,128)(2,1)} custom-call(bf16[2,64,320]{2,1,0:T(8,128)(2,1)} %bitcast.22, bf16[2,320,320]{2,1,0:T(8,128)(2,1)} %bitcast.19), custom_call_target="tpu_custom_call" | custom-call | flops 26214400 | bytes 2097152 | tf_op jit(solution)/shard_map/pallas_call | solution.py:51
  22.1 3.9 %collective-permute-start = (bf16[2,1,2,32,320]{4,3,2,1,0:T(8,128)(2,1)}, bf16[2,1,2,32,320]{4,3,2,1,0:T(8,128)(2,1)S(1)}, u32[]{:S(2)}, u32[]{:S(2)}) collective-permute-start(bf16[2,1,2,32,320]{4,3,2,1,0:T(8,128)(2,1)} %shard_map.64), channel_id=1, source_target_pairs={{0,0},{1,1},{2,32},{3,33},{4,64},{5,65},{6,96},{7,97},{8,128},{9,1... | collective-permute-start | bytes 245768 | tf_op jit(solution)/shard_map/ppermute | solution.py:107
  26.1 17.2 %collective-permute-done = bf16[2,1,2,32,320]{4,3,2,1,0:T(8,128)(2,1)S(1)} collective-permute-done((bf16[2,1,2,32,320]{4,3,2,1,0:T(8,128)(2,1)}, bf16[2,1,2,32,320]{4,3,2,1,0:T(8,128)(2,1)S(1)}, u32[]{:S(2)}, u32[]{:S(2)}) %collective-permute-start) | collective-permute-done | bytes 81952 | tf_op jit(solution)/shard_map/ppermute | solution.py:107
  43.3 0.0 all-to-all-done.1
  43.3 1.0 broadcast_in_dim.22
  44.3 16.6 %all-to-all-start = ((bf16[32,32,320]{2,1,0:T(8,128)(2,1)}), bf16[32,32,320]{2,1,0:T(8,128)(2,1)S(1)}, u32[]{:S(2)}, u32[]{:S(2)}) async-start(bf16[32,32,320]{2,1,0:T(8,128)(2,1)} %bitcast.3), calls=%async_computation | async-start | bytes 1572864 | tf_op jit(solution)/shard_map/all_to_all | solution.py:113
  60.9 0.0 copy-start.1
  60.9 17.8 %all-to-all-done = bf16[32,32,320]{2,1,0:T(8,128)(2,1)S(1)} async-done(((bf16[32,32,320]{2,1,0:T(8,128)(2,1)}), bf16[32,32,320]{2,1,0:T(8,128)(2,1)S(1)}, u32[]{:S(2)}, u32[]{:S(2)}) %all-to-all-start) | async-done | bytes 655392 | tf_op jit(solution)/shard_map/all_to_all | solution.py:113
  78.7 0.0 all-gather.3.cloned.1.call-done
  78.7 0.0 copy-start
  78.7 1.5 %copy-done = bf16[8,320,320]{2,1,0:T(8,128)(2,1)S(1)} copy-done((bf16[8,320,320]{2,1,0:T(8,128)(2,1)S(1)}, bf16[8,320,320]{2,1,0:T(8,128)(2,1)}, u32[]{:S(2)}) %copy-start) | copy-done | bytes 1638424
  80.3 2.9 %shard_map.66 = f32[16,8,128]{2,1,0:T(8,128)} custom-call(bf16[16,2,32,320]{3,2,1,0:T(8,128)(2,1)S(1)} %bitcast.16, bf16[16,2,32,320]{3,2,1,0:T(8,128)(2,1)S(1)} %bitcast.15, bf16[2,2,2,320,320]{4,3,2,1,0:T(8,128)(2,1)S(1)} %bitcast.17), custom_call_target="tpu_custom_call" | custom-call | flops 838860800 | bytes 4194304 | tf_op jit(solution)/shard_map/pallas_call | solution.py:87
  83.2 14.2 %all-to-all-start.2 = ((f32[128,1,128]{2,1,0:T(1,128)}), f32[128,1,128]{2,1,0:T(1,128)S(1)}, u32[]{:S(2)}, u32[]{:S(2)}) async-start(f32[128,1,128]{2,1,0:T(1,128)} %bitcast.11), calls=%async_computation.2 | async-start | bytes 131072 | tf_op jit(solution)/shard_map/all_to_all | solution.py:119
  97.4 0.0 copy-done.1
  97.4 12.4 %all-to-all-done.2 = f32[128,1,128]{2,1,0:T(1,128)S(1)} async-done(((f32[128,1,128]{2,1,0:T(1,128)}), f32[128,1,128]{2,1,0:T(1,128)S(1)}, u32[]{:S(2)}, u32[]{:S(2)}) %all-to-all-start.2) | async-done | bytes 65568 | tf_op jit(solution)/shard_map/all_to_all | solution.py:119
  109.8 0.2 reduce_sum.9
  109.9 0.1 reshape.83
  110.0 0.6 broadcast_select_fusion
  (1 shorter events, 0.0 us)
Async XLA Ops:
  9.0 34.3 %all-to-all-start.1 = ((bf16[32,32,320]{2,1,0:T(8,128)(2,1)}), bf16[32,32,320]{2,1,0:T(8,128)(2,1)S(1)}, u32[]{:S(2)}, u32[]{:S(2)}) async-start(bf16[32,32,320]{2,1,0:T(8,128)(2,1)} %bitcast.18), calls=%async_computation.1 | async-start | bytes 1572864 | tf_op jit(solution)/shard_map/all_to_all | solution.py:109
  19.2 59.5 %all-gather.3.cloned.1.call-start = ((), (), s32[]{:S(2)}) async-start(), calls=%async_computation.3 | async-start | bytes 2457600 | tf_op jit(solution)/shard_map/all_gather | solution.py:103
  22.1 21.2 %collective-permute-start = (bf16[2,1,2,32,320]{4,3,2,1,0:T(8,128)(2,1)}, bf16[2,1,2,32,320]{4,3,2,1,0:T(8,128)(2,1)S(1)}, u32[]{:S(2)}, u32[]{:S(2)}) collective-permute-start(bf16[2,1,2,32,320]{4,3,2,1,0:T(8,128)(2,1)} %shard_map.64), channel_id=1, source_target_pairs={{0,0},{1,1},{2,32},{3,33},{4,64},{5,65},{6,96},{7,97},{8,128},{9,1... | collective-permute-start | bytes 245768 | tf_op jit(solution)/shard_map/ppermute | solution.py:107
  44.3 34.4 %all-to-all-start = ((bf16[32,32,320]{2,1,0:T(8,128)(2,1)}), bf16[32,32,320]{2,1,0:T(8,128)(2,1)S(1)}, u32[]{:S(2)}, u32[]{:S(2)}) async-start(bf16[32,32,320]{2,1,0:T(8,128)(2,1)} %bitcast.3), calls=%async_computation | async-start | bytes 1572864 | tf_op jit(solution)/shard_map/all_to_all | solution.py:113
  60.9 36.5 %copy-start.1 = (s32[4]{0:T(128)S(1)}, s32[4]{0:T(128)}, u32[]{:S(2)}) copy-start(s32[4]{0:T(128)} %param.11) | copy-start | bytes 52
  78.7 1.5 %copy-start = (bf16[8,320,320]{2,1,0:T(8,128)(2,1)S(1)}, bf16[8,320,320]{2,1,0:T(8,128)(2,1)}, u32[]{:S(2)}) copy-start(bf16[8,320,320]{2,1,0:T(8,128)(2,1)} %all-gather.3.cloned.1.call-done) | copy-start | bytes 4915204
  83.2 26.6 %all-to-all-start.2 = ((f32[128,1,128]{2,1,0:T(1,128)}), f32[128,1,128]{2,1,0:T(1,128)S(1)}, u32[]{:S(2)}, u32[]{:S(2)}) async-start(f32[128,1,128]{2,1,0:T(1,128)} %bitcast.11), calls=%async_computation.2 | async-start | bytes 131072 | tf_op jit(solution)/shard_map/all_to_all | solution.py:119
Sparse Core Ops, SparseCore 0:
  22.1 35.3 all-gather.2

commit v2 on v1

v2 whole, which is shorter than its diff:
```python
import jax
import jax.numpy as jnp
from jax import lax
from jax.experimental import pallas as pl
from jax.experimental.pallas import tpu as pltpu
from jax.sharding import Mesh, PartitionSpec as P

AXES = ("xl", "y", "c", "z", "xh")
SIZES = (2, 8, 2, 8, 2)
NT = (((1,), (1,)), ((), ()))


def moved(to):
    _, y_n, c_n, z_n, xh_n = SIZES

    def flat(xl, y, c, z, xh):
        return (((xl * y_n + y) * c_n + c) * z_n + z) * xh_n + xh

    places = [
        (xl, y, c, z, xh)
        for xl in range(SIZES[0])
        for y in range(y_n)
        for c in range(c_n)
        for z in range(z_n)
        for xh in range(xh_n)
    ]
    return [(flat(*place), flat(*to(*place))) for place in places]


def rotate_kernel(act_ref, grad_ref, act_basis_ref, grad_basis_ref, out_ref):
    layers, tokens, _ = act_ref.shape
    half = tokens // 2
    to = lax.broadcasted_iota(jnp.int32, (tokens, tokens), 0)
    came = lax.broadcasted_iota(jnp.int32, (tokens, tokens), 1)
    wanted = jnp.where(to < half, 2 * to, 2 * (to - half) + 1)
    pick = (came == wanted).astype(jnp.bfloat16)
    for layer in range(layers):
        for kind, (rows_ref, basis_ref) in enumerate(
            ((act_ref, act_basis_ref), (grad_ref, grad_basis_ref))
        ):
            rows = jnp.dot(pick, rows_ref[layer], preferred_element_type=jnp.float32)
            turned = jnp.dot(
                rows.astype(jnp.bfloat16), basis_ref[layer], preferred_element_type=jnp.float32
            ).astype(jnp.bfloat16)
            for parity in range(2):
                out_ref[layer, parity, kind] = turned[parity * half:(parity + 1) * half]


def rotate(act_rows, grad_rows, eig_act, eig_grad):
    layers, seqs, span, width = act_rows.shape
    tokens = seqs * span
    rows, basis = (layers, tokens, width), (layers, width, width)
    return pl.pallas_call(
        rotate_kernel,
        out_shape=jax.ShapeDtypeStruct((layers, 2, 2, tokens // 2, width), jnp.bfloat16),
        cost_estimate=pl.CostEstimate(
            flops=4 * layers * tokens * width * width, bytes_accessed=2 << 20, transcendentals=0
        ),
    )(act_rows.reshape(rows), grad_rows.reshape(rows), eig_act.reshape(basis), eig_grad.reshape(basis))


def spread_kernel(rows_ref, *refs):
    out_ref = refs[-1]
    for copy in range(out_ref.shape[0]):
        out_ref[copy] = rows_ref[...]


def spread(rows, copies, after=(), flops=0):
    vmem, anywhere = pl.BlockSpec(memory_space=pltpu.VMEM), pl.BlockSpec(memory_space=pl.ANY)
    return pl.pallas_call(
        spread_kernel,
        out_shape=jax.ShapeDtypeStruct((copies,) + rows.shape, rows.dtype),
        in_specs=[vmem] + [anywhere] * len(after),
        out_specs=vmem,
        cost_estimate=pl.CostEstimate(flops=flops, bytes_accessed=1 << 20, transcendentals=0),
    )(rows, *after)


def score_kernel(place_ref, act_ref, grad_ref, *tables_and_out):
    table_refs, out_ref = tables_and_out[:-1], tables_and_out[-1]
    y_n, xl_n, _, tokens, width = act_ref.shape
    queries = table_refs[0].shape[0]
    seqs = tokens // 8
    total = y_n * tokens
    core, half = place_ref[0], place_ref[1]
    lane = lax.broadcasted_iota(jnp.int32, (y_n, 8, 128), 2)
    for xl in range(xl_n):
        out = jnp.zeros((y_n, 8, 128), jnp.float32)
        acts = [
            act_ref[:, xl, core if n == 0 else 1 - core].reshape(total, width) for n in range(2)
        ]
        grads = [
            grad_ref[:, xl, half if j == 0 else 1 - half].reshape(total, width).astype(jnp.float32)
            for j in range(2)
        ]
        for query in range(queries):
            running = jnp.zeros((total, width), jnp.float32)
            for j in range(2):
                projected = jnp.zeros((total, width), jnp.float32)
                for n in range(2):
                    projected += lax.dot_general(
                        acts[n], table_refs[2 * n + j][query], NT,
                        preferred_element_type=jnp.float32,
                    )
                running += projected * grads[j]
            column = jnp.sum(running, axis=1, keepdims=True).reshape(y_n, seqs, 8, 1)
            for seq in range(seqs):
                out = jnp.where(lane == query * seqs + seq, column[:, seq], out)
        out_ref[:, xl] = out


def score(place, act, grad, tables):
    y_n, xl_n, blocks, tokens, width = act.shape
    queries = tables[0].shape[0]
    vmem = pl.BlockSpec(memory_space=pltpu.VMEM)
    return pl.pallas_call(
        score_kernel,
        out_shape=jax.ShapeDtypeStruct((y_n, xl_n, 8, 128), jnp.float32),
        in_specs=[pl.BlockSpec(memory_space=pltpu.SMEM)] + [vmem] * (2 + len(tables)),
        out_specs=vmem,
        cost_estimate=pl.CostEstimate(
            flops=2 * y_n * xl_n * tokens * queries * (blocks * width) ** 2,
            bytes_accessed=4 << 20,
            transcendentals=0,
        ),
        compiler_params=pltpu.CompilerParams(vmem_limit_bytes=40 << 20),
    )(place, act, grad, *tables)


def per_device(act_rows, grad_rows, eig_act, eig_grad, precond, lengths):
    xl_n, y_n, _, z_n, xh_n = SIZES
    layers, seqs, span, width = act_rows.shape
    queries = precond.shape[0]
    tokens = seqs * span // 2
    place = jnp.stack([lax.axis_index("c"), lax.axis_index("xh")]).astype(jnp.int32)

    turned = rotate(act_rows, grad_rows, eig_act, eig_grad)
    turned = lax.all_to_all(
        turned.reshape(xl_n * xh_n, 2, tokens, width), ("xl", "xh"), 0, 0, tiled=True
    )
    turned, precond = lax.optimization_barrier((turned, precond))
    act = lax.ppermute(turned[:, 0], AXES, moved(lambda xl, y, c, z, xh: (xl, z, c, y, xh)))
    grad = jnp.broadcast_to(turned[:, 1], (y_n, xl_n * xh_n, tokens, width))
    grad = lax.all_to_all(grad, "y", 0, 0, tiled=True)
    other_half = lax.ppermute(precond, "xh", [(0, 1), (1, 0)])
    act = spread(act, z_n, (other_half,), 50_000_000_000)
    act = lax.all_to_all(act, "z", 0, 0, tiled=True)
    swap = [(0, 1), (1, 0)]
    tables = [precond, other_half, lax.ppermute(precond, "c", swap), lax.ppermute(other_half, "c", swap)]
    owners = (y_n, xl_n, xh_n, tokens, width)
    partial_scores = score(place, act.reshape(owners), grad.reshape(owners), tables)
    shares = lax.all_to_all(
        partial_scores.reshape(y_n * xl_n * z_n, 1, 128), ("y", "xl", "z"), 0, 0, tiled=True
    )
    summed = jnp.sum(shares, axis=(0, 1))[: queries * seqs].reshape(queries, seqs, 1)
    position = lax.axis_index(AXES)
    valid_mask = position < lengths
    return jnp.where(valid_mask[None, :, None], summed, 0.0)


def solution(mesh):
    fine = Mesh(mesh.devices.reshape(SIZES), AXES)
    dp, block = ("xl", "y", "c"), ("z", "xh")
    return jax.shard_map(
        per_device,
        mesh=fine,
        in_specs=(
            P(None, None, dp, block),
            P(None, None, dp, block),
            P(None, block, None, None),
            P(None, block, None, None),
            P(None, block, dp),
            P(),
        ),
        out_specs=P(None, None, dp + block),
        check_vma=False,
    )
```

time: 118 us -> 105 us (0.89)
  between operations: 13.5 us -> 0.13 us
  blocking collectives: 0 us -> 10.4 us
  waiting for transfers between devices: 48.1 us -> 41.7 us
  starting transfers between devices: 44.9 us -> 40.9 us
    ppermute x1 -> x4, waiting for transfers between devices: 17.2 us -> 1.38 us  [the longest x1 1.38 us: per_device(): lax.ppermute(other_half, 'c', swap)]
    all_to_all x3, starting transfers between devices: 40.9 us -> 29.2 us  [the longest x1 13.8 us: per_device(): grad = lax.all_to_all(grad, 'y', 0, 0, tiled=True)]
    all_to_all x0 -> x1, blocking collectives: none -> 10.4 us  [per_device(): lax.all_to_all(turned.reshape(xl_n * xh_n, 2, tokens, width), ('xl', 'xh'...]
    all_to_all x3, waiting for transfers between devices: 30.2 us -> 40.3 us  [the longest x1 16.7 us: per_device(): grad = lax.all_to_all(grad, 'y', 0, 0, tiled=True)]
    ppermute x1 -> x4, starting transfers between devices: 3.94 us -> 11.7 us  [the longest x1 4.16 us: per_device(): lax.ppermute(turned[:, 0], AXES, moved(lambda xl, y, c, z, xh: (xl, z, c,...]
  transfers between devices with their start and end apart: 5 -> 7, of which waited for: 3 -> 4; matrix products, arithmetic and copies ran while one was open for 1% -> 1% of each run, Pallas kernels for 2% -> 2%
where the time goes in v2:
time: 105 us
  waiting for transfers between devices  41.7 us (40%)
  starting transfers between devices  40.9 us (39%)
  blocking collectives  10.4 us (10%)
  Pallas kernels  7.5 us (7%)
  local copies, waits for them, and re-layouts  3.15 us (3%)
    all_to_all x1, waiting for transfers between devices, per_device(): grad = lax.all_to_all(grad, 'y', 0, 0, tiled=True)  16.7 us
    all_to_all x1, starting transfers between devices, per_device(): grad = lax.all_to_all(grad, 'y', 0, 0, tiled=True)  13.8 us
    all_to_all x1, waiting for transfers between devices, per_device(): lax.all_to_all(partial_scores.reshape(y_n * xl_n * z_n, 1, 128), ('y', 'x...  12.2 us
    all_to_all x1, waiting for transfers between devices, per_device(): act = lax.all_to_all(act, 'z', 0, 0, tiled=True)  11.5 us
    all_to_all x1, blocking collectives, per_device(): lax.all_to_all(turned.reshape(xl_n * xh_n, 2, tokens, width), ('xl', 'xh'...  10.4 us
    all_to_all x1, starting transfers between devices, per_device(): lax.all_to_all(partial_scores.reshape(y_n * xl_n * z_n, 1, 128), ('y', 'x...  10.3 us
    all_to_all x1, starting transfers between devices, per_device(): act = lax.all_to_all(act, 'z', 0, 0, tiled=True)  5.02 us
    ppermute x1, starting transfers between devices, per_device(): lax.ppermute(turned[:, 0], AXES, moved(lambda xl, y, c, z, xh: (xl, z, c,...  4.16 us
  transfers between devices with their start and end apart: 7, of which 4 were waited for; matrix products, arithmetic and copies ran while one was open for 1% of the time, Pallas kernels for 2%

profile of v2, /device:TPU:8, one launch (start us, length us, event | category | flops | bytes accessed | tf_op | source)
XLA Modules:
  0.0 104.7 jit_solution(7725341547709320380)
XLA Ops:
  0.0 0.0 copy-start
  0.0 2.8 %shard_map.64 = bf16[2,2,2,32,320]{4,3,2,1,0:T(8,128)(2,1)} custom-call(bf16[2,64,320]{2,1,0:T(8,128)(2,1)} %bitcast.24, bf16[2,64,320]{2,1,0:T(8,128)(2,1)} %bitcast.25, bf16[2,320,320]{2,1,0:T(8,128)(2,1)} %bitcast.22, bf16[2,320,320]{2,1,0:T(8,128)(2,1)} %bitcast.23), custom_call_target="tpu_custom_call" | custom-call | flops 52428800 | bytes 2097152 | tf_op jit(solution)/shard_map/pallas_call | solution.py:53
  2.8 10.4 %all_to_all.20 = bf16[4,2,32,320]{3,2,1,0:T(8,128)(2,1)S(1)} all-to-all(bf16[4,2,32,320]{3,2,1,0:T(8,128)(2,1)} %bitcast.21), channel_id=1, replica_groups=mesh['xl'=2,'y'=8,'c'=2,'z'=8,'xh'=2] {'xl','xh'}, dimensions={0} | all-to-all | bytes 327680 | tf_op jit(solution)/shard_map/all_to_all | solution.py:138
  13.2 0.0 copy-done
  13.2 3.2 %collective-permute-start.1 = (bf16[2,320,320]{2,1,0:T(8,128)(2,1)S(1)}, bf16[2,320,320]{2,1,0:T(8,128)(2,1)S(1)}, u32[]{:S(2)}, u32[]{:S(2)}) collective-permute-start(bf16[2,320,320]{2,1,0:T(8,128)(2,1)S(1)} %copy-done), channel_id=1, source_target_pairs={{0,1},{1,0},{2,3},{3,2},{4,5},{5,4},{6,7},{7,6},{8,9},{9,8},{10,11... | collective-permute-start | bytes 1228808 | tf_op jit(solution)/shard_map/ppermute | solution.py:145
  16.5 4.2 %collective-permute-start = (bf16[4,32,320]{2,1,0:T(8,128)(2,1)S(1)}, bf16[4,32,320]{2,1,0:T(8,128)(2,1)S(1)}, u32[]{:S(2)}, u32[]{:S(2)}) collective-permute-start(bf16[4,32,320]{2,1,0:T(8,128)(2,1)S(1)} %slice_bitcast_fusion), channel_id=1, source_target_pairs={{0,0},{1,1},{2,32},{3,33},{4,64},{5,65},{6,96},{7,97},{8,128},{9,1... | collective-permute-start | bytes 245768 | tf_op jit(solution)/shard_map/ppermute | solution.py:142
  20.7 1.0 broadcast_in_dim.17
  21.7 13.8 %all-to-all-start.2 = ((bf16[8,4,32,320]{3,2,1,0:T(8,128)(2,1)}), bf16[8,4,32,320]{3,2,1,0:T(8,128)(2,1)S(1)}, u32[]{:S(2)}, u32[]{:S(2)}) async-start(bf16[8,4,32,320]{3,2,1,0:T(8,128)(2,1)} %broadcast_in_dim.17), calls=%async_computation.2 | async-start | bytes 1572864 | tf_op jit(solution)/shard_map/all_to_all | solution.py:144
  35.6 0.0 collective-permute-done.rows_ref
  35.6 0.0 copy-start.4
  35.6 0.0 collective-permute-done.1.refs_0_.tables_and_out_1_
  35.6 0.6 copy-done.4
  36.2 0.8 copy-done.1
  37.0 1.9 %shard_map.65 = bf16[8,4,32,320]{3,2,1,0:T(8,128)(2,1)} custom-call(bf16[4,32,320]{2,1,0:T(8,128)(2,1)} %copy-done.4, bf16[2,320,320]{2,1,0:T(8,128)(2,1)} %copy-done.1), custom_call_target="tpu_custom_call" | custom-call | flops 49999998976 | bytes 1048576 | tf_op jit(solution)/shard_map/pallas_call | solution.py:70
  38.8 16.7 %all-to-all-done.2 = bf16[8,4,32,320]{3,2,1,0:T(8,128)(2,1)S(1)} async-done(((bf16[8,4,32,320]{3,2,1,0:T(8,128)(2,1)}), bf16[8,4,32,320]{3,2,1,0:T(8,128)(2,1)S(1)}, u32[]{:S(2)}, u32[]{:S(2)}) %all-to-all-start.2) | async-done | bytes 655392 | tf_op jit(solution)/shard_map/all_to_all | solution.py:144
  55.5 5.0 %all-to-all-start.1 = ((bf16[8,4,32,320]{3,2,1,0:T(8,128)(2,1)}), bf16[8,4,32,320]{3,2,1,0:T(8,128)(2,1)S(1)}, u32[]{:S(2)}, u32[]{:S(2)}) async-start(bf16[8,4,32,320]{3,2,1,0:T(8,128)(2,1)} %shard_map.65), calls=%async_computation.1 | async-start | bytes 1572864 | tf_op jit(solution)/shard_map/all_to_all | solution.py:147
  60.5 1.9 %collective-permute-start.2 = (bf16[2,320,320]{2,1,0:T(8,128)(2,1)S(1)}, bf16[2,320,320]{2,1,0:T(8,128)(2,1)S(1)}, u32[]{:S(2)}, u32[]{:S(2)}) collective-permute-start(bf16[2,320,320]{2,1,0:T(8,128)(2,1)S(1)} %copy-done), channel_id=1, source_target_pairs={{0,16},{16,0},{1,17},{17,1},{2,18},{18,2},{3,19},{19,3},{4,20},{20... | collective-permute-start | bytes 1228808 | tf_op jit(solution)/shard_map/ppermute | solution.py:149
  62.5 0.0 copy-done.2
  62.5 2.4 %collective-permute-start.3 = (bf16[2,320,320]{2,1,0:T(8,128)(2,1)S(1)}, bf16[2,320,320]{2,1,0:T(8,128)(2,1)S(1)}, u32[]{:S(2)}, u32[]{:S(2)}) collective-permute-start(bf16[2,320,320]{2,1,0:T(8,128)(2,1)S(1)} %copy-done.2), channel_id=1, source_target_pairs={{0,16},{16,0},{1,17},{17,1},{2,18},{18,2},{3,19},{19,3},{4,20},{20... | collective-permute-start | bytes 1228808 | tf_op jit(solution)/shard_map/ppermute | solution.py:149
  64.9 0.1 pad_add_fusion.place_ref
  65.0 0.0 collective-permute-done.2.tables_and_out_2_
  65.0 1.4 %collective-permute-done.3.tables_and_out_3_ = bf16[2,320,320]{2,1,0:T(8,128)(2,1)S(1)} collective-permute-done((bf16[2,320,320]{2,1,0:T(8,128)(2,1)S(1)}, bf16[2,320,320]{2,1,0:T(8,128)(2,1)S(1)}, u32[]{:S(2)}, u32[]{:S(2)}) %collective-permute-start.3) | collective-permute-done | bytes 409632 | tf_op jit(solution)/shard_map/ppermute | solution.py:149
  66.4 11.5 %all-to-all-done.1 = bf16[8,4,32,320]{3,2,1,0:T(8,128)(2,1)S(1)} async-done(((bf16[8,4,32,320]{3,2,1,0:T(8,128)(2,1)}), bf16[8,4,32,320]{3,2,1,0:T(8,128)(2,1)S(1)}, u32[]{:S(2)}, u32[]{:S(2)}) %all-to-all-start.1) | async-done | bytes 655392 | tf_op jit(solution)/shard_map/all_to_all | solution.py:147
  77.8 2.9 %shard_map.66 = f32[8,2,8,128]{3,2,1,0:T(8,128)S(1)} custom-call(s32[2]{0:T(128)S(1)} %pad_add_fusion.place_ref, bf16[8,2,2,32,320]{4,3,2,1,0:T(8,128)(2,1)S(1)} %bitcast.19, bf16[8,2,2,32,320]{4,3,2,1,0:T(8,128)(2,1)S(1)} %bitcast.18, bf16[2,320,320]{2,1,0:T(8,128)(2,1)S(1)} %copy-done, bf16[2,320,320]{2,1,0:T(8,128)(2,1)S(1)} %copy-done.2, ...), custom_call_target="tpu_custom_call" | custom-call | flops 838860800 | bytes 4194304 | tf_op jit(solution)/shard_map/pallas_call | solution.py:116
  80.7 0.0 copy-start.3
  80.7 0.6 copy-done.3
  81.3 10.3 %all-to-all-start.3 = ((f32[128,1,128]{2,1,0:T(1,128)}), f32[128,1,128]{2,1,0:T(1,128)S(1)}, u32[]{:S(2)}, u32[]{:S(2)}) async-start(f32[128,1,128]{2,1,0:T(1,128)} %bitcast.20), calls=%async_computation.3 | async-start | bytes 131072 | tf_op jit(solution)/shard_map/all_to_all | solution.py:152
  91.7 0.0 copy-done.5
  91.7 12.2 %all-to-all-done.3 = f32[128,1,128]{2,1,0:T(1,128)S(1)} async-done(((f32[128,1,128]{2,1,0:T(1,128)}), f32[128,1,128]{2,1,0:T(1,128)S(1)}, u32[]{:S(2)}, u32[]{:S(2)}) %all-to-all-start.3) | async-done | bytes 65568 | tf_op jit(solution)/shard_map/all_to_all | solution.py:152
  103.8 0.2 reduce_sum.9
  104.0 0.1 reshape.75
  104.1 0.6 broadcast_select_fusion
  (6 shorter events, 0.0 us)
Async XLA Ops:
  0.0 13.2 %copy-start = (bf16[2,320,320]{2,1,0:T(8,128)(2,1)S(1)}, bf16[2,320,320]{2,1,0:T(8,128)(2,1)}, u32[]{:S(2)}) copy-start(bf16[2,320,320]{2,1,0:T(8,128)(2,1)} %tables_and_out_0_) | copy-start | bytes 1228804
  13.2 22.3 %collective-permute-start.1 = (bf16[2,320,320]{2,1,0:T(8,128)(2,1)S(1)}, bf16[2,320,320]{2,1,0:T(8,128)(2,1)S(1)}, u32[]{:S(2)}, u32[]{:S(2)}) collective-permute-start(bf16[2,320,320]{2,1,0:T(8,128)(2,1)S(1)} %copy-done), channel_id=1, source_target_pairs={{0,1},{1,0},{2,3},{3,2},{4,5},{5,4},{6,7},{7,6},{8,9},{9,8},{10,11... | collective-permute-start | bytes 1228808 | tf_op jit(solution)/shard_map/ppermute | solution.py:145
  16.5 19.0 %collective-permute-start = (bf16[4,32,320]{2,1,0:T(8,128)(2,1)S(1)}, bf16[4,32,320]{2,1,0:T(8,128)(2,1)S(1)}, u32[]{:S(2)}, u32[]{:S(2)}) collective-permute-start(bf16[4,32,320]{2,1,0:T(8,128)(2,1)S(1)} %slice_bitcast_fusion), channel_id=1, source_target_pairs={{0,0},{1,1},{2,32},{3,33},{4,64},{5,65},{6,96},{7,97},{8,128},{9,1... | collective-permute-start | bytes 245768 | tf_op jit(solution)/shard_map/ppermute | solution.py:142
  21.7 33.8 %all-to-all-start.2 = ((bf16[8,4,32,320]{3,2,1,0:T(8,128)(2,1)}), bf16[8,4,32,320]{3,2,1,0:T(8,128)(2,1)S(1)}, u32[]{:S(2)}, u32[]{:S(2)}) async-start(bf16[8,4,32,320]{3,2,1,0:T(8,128)(2,1)} %broadcast_in_dim.17), calls=%async_computation.2 | async-start | bytes 1572864 | tf_op jit(solution)/shard_map/all_to_all | solution.py:144
  35.6 0.6 copy-start.4
  36.2 0.8 copy-start.1
  38.8 23.6 %copy-start.2 = (bf16[2,320,320]{2,1,0:T(8,128)(2,1)S(1)}, bf16[2,320,320]{2,1,0:T(8,128)(2,1)}, u32[]{:S(2)}) copy-start(bf16[2,320,320]{2,1,0:T(8,128)(2,1)} %copy-done.1) | copy-start | bytes 1228804
  55.5 22.3 %all-to-all-start.1 = ((bf16[8,4,32,320]{3,2,1,0:T(8,128)(2,1)}), bf16[8,4,32,320]{3,2,1,0:T(8,128)(2,1)S(1)}, u32[]{:S(2)}, u32[]{:S(2)}) async-start(bf16[8,4,32,320]{3,2,1,0:T(8,128)(2,1)} %shard_map.65), calls=%async_computation.1 | async-start | bytes 1572864 | tf_op jit(solution)/shard_map/all_to_all | solution.py:147
  60.5 4.4 %collective-permute-start.2 = (bf16[2,320,320]{2,1,0:T(8,128)(2,1)S(1)}, bf16[2,320,320]{2,1,0:T(8,128)(2,1)S(1)}, u32[]{:S(2)}, u32[]{:S(2)}) collective-permute-start(bf16[2,320,320]{2,1,0:T(8,128)(2,1)S(1)} %copy-done), channel_id=1, source_target_pairs={{0,16},{16,0},{1,17},{17,1},{2,18},{18,2},{3,19},{19,3},{4,20},{20... | collective-permute-start | bytes 1228808 | tf_op jit(solution)/shard_map/ppermute | solution.py:149
  62.5 3.9 %collective-permute-start.3 = (bf16[2,320,320]{2,1,0:T(8,128)(2,1)S(1)}, bf16[2,320,320]{2,1,0:T(8,128)(2,1)S(1)}, u32[]{:S(2)}, u32[]{:S(2)}) collective-permute-start(bf16[2,320,320]{2,1,0:T(8,128)(2,1)S(1)} %copy-done.2), channel_id=1, source_target_pairs={{0,16},{16,0},{1,17},{17,1},{2,18},{18,2},{3,19},{19,3},{4,20},{20... | collective-permute-start | bytes 1228808 | tf_op jit(solution)/shard_map/ppermute | solution.py:149
  80.7 0.6 copy-start.3
  81.3 10.3 %copy-start.5 = (s32[4]{0:T(128)S(1)}, s32[4]{0:T(128)}, u32[]{:S(2)}) copy-start(s32[4]{0:T(128)} %param.11) | copy-start | bytes 52
  81.3 22.5 %all-to-all-start.3 = ((f32[128,1,128]{2,1,0:T(1,128)}), f32[128,1,128]{2,1,0:T(1,128)S(1)}, u32[]{:S(2)}, u32[]{:S(2)}) async-start(f32[128,1,128]{2,1,0:T(1,128)} %bitcast.20), calls=%async_computation.3 | async-start | bytes 131072 | tf_op jit(solution)/shard_map/all_to_all | solution.py:152

commit v3 on v2

--- a/solution.py
+++ b/solution.py
@@ -59,21 +59,22 @@
     )(act_rows.reshape(rows), grad_rows.reshape(rows), eig_act.reshape(basis), eig_grad.reshape(basis))
 
 
-def spread_kernel(rows_ref, *refs):
-    out_ref = refs[-1]
-    for copy in range(out_ref.shape[0]):
-        out_ref[copy] = rows_ref[...]
+def hold_kernel(rows_ref, out_ref):
+    pass
 
 
-def spread(rows, copies, after=(), flops=0):
-    vmem, anywhere = pl.BlockSpec(memory_space=pltpu.VMEM), pl.BlockSpec(memory_space=pl.ANY)
+def hold(rows):
+    anywhere = pl.BlockSpec(memory_space=pl.ANY)
     return pl.pallas_call(
-        spread_kernel,
-        out_shape=jax.ShapeDtypeStruct((copies,) + rows.shape, rows.dtype),
-        in_specs=[vmem] + [anywhere] * len(after),
-        out_specs=vmem,
-        cost_estimate=pl.CostEstimate(flops=flops, bytes_accessed=1 << 20, transcendentals=0),
-    )(rows, *after)
+        hold_kernel,
+        out_shape=jax.ShapeDtypeStruct(rows.shape, rows.dtype),
+        in_specs=[anywhere],
+        out_specs=anywhere,
+        input_output_aliases={0: 0},
+        cost_estimate=pl.CostEstimate(
+            flops=50_000_000_000, bytes_accessed=0, transcendentals=0
+        ),
+    )(rows)
 
 
 def score_kernel(place_ref, act_ref, grad_ref, *tables_and_out):
@@ -128,26 +129,27 @@
 
 
 def per_device(act_rows, grad_rows, eig_act, eig_grad, precond, lengths):
-    xl_n, y_n, _, z_n, xh_n = SIZES
+    xl_n, y_n, c_n, z_n, xh_n = SIZES
     layers, seqs, span, width = act_rows.shape
     queries = precond.shape[0]
     tokens = seqs * span // 2
+    swap = [(0, 1), (1, 0)]
     place = jnp.stack([lax.axis_index("c"), lax.axis_index("xh")]).astype(jnp.int32)
+    other_core = lax.ppermute(precond, "c", swap)
 
     turned = rotate(act_rows, grad_rows, eig_act, eig_grad)
     turned = lax.all_to_all(
         turned.reshape(xl_n * xh_n, 2, tokens, width), ("xl", "xh"), 0, 0, tiled=True
     )
-    turned, precond = lax.optimization_barrier((turned, precond))
     act = lax.ppermute(turned[:, 0], AXES, moved(lambda xl, y, c, z, xh: (xl, z, c, y, xh)))
     grad = jnp.broadcast_to(turned[:, 1], (y_n, xl_n * xh_n, tokens, width))
     grad = lax.all_to_all(grad, "y", 0, 0, tiled=True)
-    other_half = lax.ppermute(precond, "xh", [(0, 1), (1, 0)])
-    act = spread(act, z_n, (other_half,), 50_000_000_000)
-    act = lax.all_to_all(act, "z", 0, 0, tiled=True)
-    swap = [(0, 1), (1, 0)]
-    tables = [precond, other_half, lax.ppermute(precond, "c", swap), lax.ppermute(other_half, "c", swap)]
+    act = lax.all_gather(hold(act), "z", axis=0, tiled=False)
     owners = (y_n, xl_n, xh_n, tokens, width)
+    tables = [
+        precond, lax.ppermute(precond, "xh", swap),
+        other_core, lax.ppermute(other_core, "xh", swap),
+    ]
     partial_scores = score(place, act.reshape(owners), grad.reshape(owners), tables)
     shares = lax.all_to_all(
         partial_scores.reshape(y_n * xl_n * z_n, 1, 128), ("y", "xl", "z"), 0, 0, tiled=True

time: 105 us -> 93.4 us (0.89)
  the two profiles are of different devices: /device:TPU:8 before, /device:TPU:4 now
where the time goes in v3:
time: 93.4 us; the launch traced here: 93 us
  starting transfers between devices  45 us (48%)
  blocking collectives  26.3 us (28%)
  waiting for transfers between devices  12.7 us (14%)
  Pallas kernels  5.68 us (6%)
  local copies, waits for them, and re-layouts  2.34 us (3%)
    all_gather x1, blocking collectives, per_device(): act = lax.all_gather(hold(act), 'z', axis=0, tiled=False)  26.3 us
    all_to_all x1, starting transfers between devices, per_device(): lax.all_to_all(partial_scores.reshape(y_n * xl_n * z_n, 1, 128), ('y', 'x...  13.4 us
    all_to_all x1, waiting for transfers between devices, per_device(): lax.all_to_all(partial_scores.reshape(y_n * xl_n * z_n, 1, 128), ('y', 'x...  12.6 us
    all_to_all x1, starting transfers between devices, per_device(): grad = lax.all_to_all(grad, 'y', 0, 0, tiled=True)  12.5 us
    all_to_all x1, starting transfers between devices, per_device(): lax.all_to_all(turned.reshape(xl_n * xh_n, 2, tokens, width), ('xl', 'xh'...  9.21 us
    ppermute x1, starting transfers between devices, per_device(): lax.ppermute(other_core, 'xh', swap)  5.34 us
    pallas_call x1, Pallas kernels, score(): pl.pallas_call(score_kernel, out_shape=jax.ShapeDtypeStruct((y_n, xl_n, 8...  2.89 us
    pallas_call x1, Pallas kernels, rotate(): pl.pallas_call(rotate_kernel, out_shape=jax.ShapeDtypeStruct((layers, 2,...  2.79 us
  transfers between devices with their start and end apart: 7, of which 2 were waited for; matrix products, arithmetic and copies ran while one was open for 1% of the time, Pallas kernels for 0%

profile of v3, /device:TPU:4, one launch (start us, length us, event | category | flops | bytes accessed | tf_op | source)
XLA Modules:
  0.0 93.0 jit_solution(17345044016452424098)
XLA Ops:
  0.0 0.0 copy-start
  0.0 2.8 %shard_map.64 = bf16[2,2,2,32,320]{4,3,2,1,0:T(8,128)(2,1)} custom-call(bf16[2,64,320]{2,1,0:T(8,128)(2,1)} %bitcast.26, bf16[2,64,320]{2,1,0:T(8,128)(2,1)} %bitcast.27, bf16[2,320,320]{2,1,0:T(8,128)(2,1)} %bitcast.24, bf16[2,320,320]{2,1,0:T(8,128)(2,1)} %bitcast.25), custom_call_target="tpu_custom_call" | custom-call | flops 52428800 | bytes 2097152 | tf_op jit(solution)/shard_map/pallas_call | solution.py:53
  2.8 9.2 %all-to-all-start = ((bf16[4,2,32,320]{3,2,1,0:T(8,128)(2,1)}), bf16[4,2,32,320]{3,2,1,0:T(8,128)(2,1)S(1)}, u32[]{:S(2)}, u32[]{:S(2)}) async-start(bf16[4,2,32,320]{3,2,1,0:T(8,128)(2,1)} %bitcast.23), calls=%async_computation | async-start | bytes 393216 | tf_op jit(solution)/shard_map/all_to_all | solution.py:141
  12.0 0.0 copy-done
  12.0 1.9 %collective-permute-start.2 = (bf16[2,320,320]{2,1,0:T(8,128)(2,1)S(1)}, bf16[2,320,320]{2,1,0:T(8,128)(2,1)S(1)}, u32[]{:S(2)}, u32[]{:S(2)}) collective-permute-start(bf16[2,320,320]{2,1,0:T(8,128)(2,1)S(1)} %copy-done), channel_id=1, source_target_pairs={{0,16},{16,0},{1,17},{17,1},{2,18},{18,2},{3,19},{19,3},{4,20},{20... | collective-permute-start | bytes 1228808 | tf_op jit(solution)/shard_map/ppermute | solution.py:138
  13.9 2.0 %collective-permute-start.1 = (bf16[2,320,320]{2,1,0:T(8,128)(2,1)S(1)}, bf16[2,320,320]{2,1,0:T(8,128)(2,1)S(1)}, u32[]{:S(2)}, u32[]{:S(2)}) collective-permute-start(bf16[2,320,320]{2,1,0:T(8,128)(2,1)S(1)} %copy-done), channel_id=1, source_target_pairs={{0,1},{1,0},{2,3},{3,2},{4,5},{5,4},{6,7},{7,6},{8,9},{9,8},{10,11... | collective-permute-start | bytes 1228808 | tf_op jit(solution)/shard_map/ppermute | solution.py:150
  15.9 0.1 all-to-all-done
  16.0 0.7 collective-permute-start
  16.7 0.1 pad_add_fusion.place_ref
  16.8 1.0 %broadcast_in_dim.17 = bf16[8,4,32,320]{3,2,1,0:T(8,128)(2,1)} broadcast(bf16[4,32,320]{2,1,0:T(8,128)(2,1)S(1)} %get-tuple-element.5), dimensions={1,2,3} | broadcast | bytes 737280 | tf_op jit(solution)/shard_map/broadcast_in_dim | solution.py:145
  17.7 12.5 %all-to-all-start.1 = ((bf16[8,4,32,320]{3,2,1,0:T(8,128)(2,1)}), bf16[8,4,32,320]{3,2,1,0:T(8,128)(2,1)S(1)}, u32[]{:S(2)}, u32[]{:S(2)}) async-start(bf16[8,4,32,320]{3,2,1,0:T(8,128)(2,1)} %broadcast_in_dim.17), calls=%async_computation.1 | async-start | bytes 1572864 | tf_op jit(solution)/shard_map/all_to_all | solution.py:146
  30.2 0.0 collective-permute-done.2.tables_and_out_2_
  30.2 5.3 %collective-permute-start.3 = (bf16[2,320,320]{2,1,0:T(8,128)(2,1)S(1)}, bf16[2,320,320]{2,1,0:T(8,128)(2,1)S(1)}, u32[]{:S(2)}, u32[]{:S(2)}) collective-permute-start(bf16[2,320,320]{2,1,0:T(8,128)(2,1)S(1)} %collective-permute-done.2.tables_and_out_2_), channel_id=1, source_target_pairs={{0,1},{1,0},{2,3},{3,2},{4,5},{5,4},{6,7},{7,6},{8,9},{9,8},{10,11... | collective-permute-start | bytes 1228808 | tf_op jit(solution)/shard_map/ppermute | solution.py:151
  35.6 0.0 collective-permute-done.rows_ref
  35.6 0.0 copy-start.2
  35.6 0.6 copy-done.2
  36.2 26.3 %all-gather = bf16[32,32,320]{2,1,0:T(8,128)(2,1)S(1)} all-gather(bf16[4,32,320]{2,1,0:T(8,128)(2,1)} %shard_map.65), channel_id=2, replica_groups=mesh['xl'=2,'y'=8,'c'=2,'z'=8,'xh'=2] {'z'}, dimensions={0}, use_global_device_ids=true | all-gather | bytes 737280 | tf_op jit(solution)/shard_map/all_gather | solution.py:147
  62.5 0.0 collective-permute-done.1.tables_and_out_1_
  62.5 0.0 collective-permute-done.3.tables_and_out_3_
  62.5 0.0 all-to-all-done.1
  62.5 2.9 %shard_map.66 = f32[8,2,8,128]{3,2,1,0:T(8,128)S(1)} custom-call(s32[2]{0:T(128)S(1)} %pad_add_fusion.place_ref, bf16[8,2,2,32,320]{4,3,2,1,0:T(8,128)(2,1)S(1)} %bitcast.21, bf16[8,2,2,32,320]{4,3,2,1,0:T(8,128)(2,1)S(1)} %bitcast.20, bf16[2,320,320]{2,1,0:T(8,128)(2,1)S(1)} %copy-done, bf16[2,320,320]{2,1,0:T(8,128)(2,1)S(1)} %collective-permute-done.1.tables_and_out_1_, ...), custom_call_target="tpu_custom_call" | custom-call | flops 838860800 | bytes 4194304 | tf_op jit(solution)/shard_map/pallas_call | solution.py:117
  65.4 0.0 copy-start.1
  65.4 0.6 copy-done.1
  66.0 0.0 copy-start.3
  66.0 13.4 %all-to-all-start.2 = ((f32[128,1,128]{2,1,0:T(1,128)}), f32[128,1,128]{2,1,0:T(1,128)S(1)}, u32[]{:S(2)}, u32[]{:S(2)}) async-start(f32[128,1,128]{2,1,0:T(1,128)} %bitcast.22), calls=%async_computation.2 | async-start | bytes 131072 | tf_op jit(solution)/shard_map/all_to_all | solution.py:154
  79.5 0.0 copy-done.3
  79.5 12.6 %all-to-all-done.2 = f32[128,1,128]{2,1,0:T(1,128)S(1)} async-done(((f32[128,1,128]{2,1,0:T(1,128)}), f32[128,1,128]{2,1,0:T(1,128)S(1)}, u32[]{:S(2)}, u32[]{:S(2)}) %all-to-all-start.2) | async-done | bytes 65568 | tf_op jit(solution)/shard_map/all_to_all | solution.py:154
  92.2 0.2 reduce_sum.9
  92.3 0.1 reshape.75
  92.4 0.6 broadcast_select_fusion
  (3 shorter events, 0.0 us)
Async XLA Ops:
  0.0 12.0 %copy-start = (bf16[2,320,320]{2,1,0:T(8,128)(2,1)S(1)}, bf16[2,320,320]{2,1,0:T(8,128)(2,1)}, u32[]{:S(2)}) copy-start(bf16[2,320,320]{2,1,0:T(8,128)(2,1)} %tables_and_out_0_.1) | copy-start | bytes 1228804
  2.8 13.2 %all-to-all-start = ((bf16[4,2,32,320]{3,2,1,0:T(8,128)(2,1)}), bf16[4,2,32,320]{3,2,1,0:T(8,128)(2,1)S(1)}, u32[]{:S(2)}, u32[]{:S(2)}) async-start(bf16[4,2,32,320]{3,2,1,0:T(8,128)(2,1)} %bitcast.23), calls=%async_computation | async-start | bytes 393216 | tf_op jit(solution)/shard_map/all_to_all | solution.py:141
  12.0 18.2 %collective-permute-start.2 = (bf16[2,320,320]{2,1,0:T(8,128)(2,1)S(1)}, bf16[2,320,320]{2,1,0:T(8,128)(2,1)S(1)}, u32[]{:S(2)}, u32[]{:S(2)}) collective-permute-start(bf16[2,320,320]{2,1,0:T(8,128)(2,1)S(1)} %copy-done), channel_id=1, source_target_pairs={{0,16},{16,0},{1,17},{17,1},{2,18},{18,2},{3,19},{19,3},{4,20},{20... | collective-permute-start | bytes 1228808 | tf_op jit(solution)/shard_map/ppermute | solution.py:138
  13.9 48.6 %collective-permute-start.1 = (bf16[2,320,320]{2,1,0:T(8,128)(2,1)S(1)}, bf16[2,320,320]{2,1,0:T(8,128)(2,1)S(1)}, u32[]{:S(2)}, u32[]{:S(2)}) collective-permute-start(bf16[2,320,320]{2,1,0:T(8,128)(2,1)S(1)} %copy-done), channel_id=1, source_target_pairs={{0,1},{1,0},{2,3},{3,2},{4,5},{5,4},{6,7},{7,6},{8,9},{9,8},{10,11... | collective-permute-start | bytes 1228808 | tf_op jit(solution)/shard_map/ppermute | solution.py:150
  16.0 19.6 %collective-permute-start = (bf16[4,32,320]{2,1,0:T(8,128)(2,1)S(1)}, bf16[4,32,320]{2,1,0:T(8,128)(2,1)S(1)}, u32[]{:S(2)}, u32[]{:S(2)}) collective-permute-start(bf16[4,32,320]{2,1,0:T(8,128)(2,1)S(1)} %get-tuple-element.6), channel_id=1, source_target_pairs={{0,0},{1,1},{2,32},{3,33},{4,64},{5,65},{6,96},{7,97},{8,128},{9,1... | collective-permute-start | bytes 245768 | tf_op jit(solution)/shard_map/ppermute | solution.py:144
  17.7 44.8 %all-to-all-start.1 = ((bf16[8,4,32,320]{3,2,1,0:T(8,128)(2,1)}), bf16[8,4,32,320]{3,2,1,0:T(8,128)(2,1)S(1)}, u32[]{:S(2)}, u32[]{:S(2)}) async-start(bf16[8,4,32,320]{3,2,1,0:T(8,128)(2,1)} %broadcast_in_dim.17), calls=%async_computation.1 | async-start | bytes 1572864 | tf_op jit(solution)/shard_map/all_to_all | solution.py:146
  30.2 32.3 %collective-permute-start.3 = (bf16[2,320,320]{2,1,0:T(8,128)(2,1)S(1)}, bf16[2,320,320]{2,1,0:T(8,128)(2,1)S(1)}, u32[]{:S(2)}, u32[]{:S(2)}) collective-permute-start(bf16[2,320,320]{2,1,0:T(8,128)(2,1)S(1)} %collective-permute-done.2.tables_and_out_2_), channel_id=1, source_target_pairs={{0,1},{1,0},{2,3},{3,2},{4,5},{5,4},{6,7},{7,6},{8,9},{9,8},{10,11... | collective-permute-start | bytes 1228808 | tf_op jit(solution)/shard_map/ppermute | solution.py:151
  35.6 0.6 copy-start.2
  65.4 0.6 copy-start.1
  66.0 13.5 %copy-start.3 = (s32[4]{0:T(128)S(1)}, s32[4]{0:T(128)}, u32[]{:S(2)}) copy-start(s32[4]{0:T(128)} %param.11) | copy-start | bytes 52
  66.0 26.1 %all-to-all-start.2 = ((f32[128,1,128]{2,1,0:T(1,128)}), f32[128,1,128]{2,1,0:T(1,128)S(1)}, u32[]{:S(2)}, u32[]{:S(2)}) async-start(f32[128,1,128]{2,1,0:T(1,128)} %bitcast.22), calls=%async_computation.2 | async-start | bytes 131072 | tf_op jit(solution)/shard_map/all_to_all | solution.py:154

commit v4 on v3

--- a/solution.py
+++ b/solution.py
@@ -27,23 +27,22 @@
     return [(flat(*place), flat(*to(*place))) for place in places]
 
 
-def rotate_kernel(act_ref, grad_ref, act_basis_ref, grad_basis_ref, out_ref):
-    layers, tokens, _ = act_ref.shape
+def rotate_kernel(act_ref, grad_ref, act_basis_ref, grad_basis_ref, out_ref, turned_ref):
+    layers, tokens, width = act_ref.shape
     half = tokens // 2
-    to = lax.broadcasted_iota(jnp.int32, (tokens, tokens), 0)
-    came = lax.broadcasted_iota(jnp.int32, (tokens, tokens), 1)
-    wanted = jnp.where(to < half, 2 * to, 2 * (to - half) + 1)
-    pick = (came == wanted).astype(jnp.bfloat16)
     for layer in range(layers):
         for kind, (rows_ref, basis_ref) in enumerate(
             ((act_ref, act_basis_ref), (grad_ref, grad_basis_ref))
         ):
-            rows = jnp.dot(pick, rows_ref[layer], preferred_element_type=jnp.float32)
-            turned = jnp.dot(
-                rows.astype(jnp.bfloat16), basis_ref[layer], preferred_element_type=jnp.float32
-            ).astype(jnp.bfloat16)
-            for parity in range(2):
-                out_ref[layer, parity, kind] = turned[parity * half:(parity + 1) * half]
+            turned = jnp.dot(rows_ref[layer], basis_ref[layer], preferred_element_type=jnp.float32)
+            for piece in range(turned_ref.shape[2]):
+                start, size = 128 * piece, min(128, width - 128 * piece)
+                turned_ref[layer, kind, piece, :, :size] = turned[:, start:start + size]
+                for parity in range(2):
+                    rows = turned_ref[layer, kind, piece, pl.ds(parity, half, 2), :]
+                    out_ref[layer, parity, kind, :, start:start + size] = (
+                        rows[:, :size].astype(jnp.bfloat16)
+                    )
 
 
 def rotate(act_rows, grad_rows, eig_act, eig_grad):
@@ -53,6 +52,7 @@
     return pl.pallas_call(
         rotate_kernel,
         out_shape=jax.ShapeDtypeStruct((layers, 2, 2, tokens // 2, width), jnp.bfloat16),
+        scratch_shapes=[pltpu.VMEM((layers, 2, pl.cdiv(width, 128), tokens, 128), jnp.float32)],
         cost_estimate=pl.CostEstimate(
             flops=4 * layers * tokens * width * width, bytes_accessed=2 << 20, transcendentals=0
         ),
@@ -135,7 +135,7 @@
     tokens = seqs * span // 2
     swap = [(0, 1), (1, 0)]
     place = jnp.stack([lax.axis_index("c"), lax.axis_index("xh")]).astype(jnp.int32)
-    other_core = lax.ppermute(precond, "c", swap)
+    other_half = lax.ppermute(precond, "xh", swap)
 
     turned = rotate(act_rows, grad_rows, eig_act, eig_grad)
     turned = lax.all_to_all(
@@ -147,8 +147,7 @@
     act = lax.all_gather(hold(act), "z", axis=0, tiled=False)
     owners = (y_n, xl_n, xh_n, tokens, width)
     tables = [
-        precond, lax.ppermute(precond, "xh", swap),
-        other_core, lax.ppermute(other_core, "xh", swap),
+        precond, other_half, lax.ppermute(precond, "c", swap), lax.ppermute(other_half, "c", swap),
     ]
     partial_scores = score(place, act.reshape(owners), grad.reshape(owners), tables)
     shares = lax.all_to_all(

time: 93.4 us -> 90.8 us (0.972)
  the two profiles are of different devices: /device:TPU:4 before, /device:TPU:8 now
where the time goes in v4:
time: 90.8 us; the launch traced here: 90.3 us
  starting transfers between devices  42.2 us (46%)
  blocking collectives  27.5 us (30%)
  waiting for transfers between devices  12.1 us (13%)
  Pallas kernels  5.21 us (6%)
  local copies, waits for them, and re-layouts  2.34 us (3%)
    all_gather x1, blocking collectives, per_device(): act = lax.all_gather(hold(act), 'z', axis=0, tiled=False)  27.5 us
    all_to_all x1, starting transfers between devices, per_device(): grad = lax.all_to_all(grad, 'y', 0, 0, tiled=True)  13.8 us
    all_to_all x1, waiting for transfers between devices, per_device(): lax.all_to_all(partial_scores.reshape(y_n * xl_n * z_n, 1, 128), ('y', 'x...  12.1 us
    all_to_all x1, starting transfers between devices, per_device(): lax.all_to_all(partial_scores.reshape(y_n * xl_n * z_n, 1, 128), ('y', 'x...  10.6 us
    ppermute x1, starting transfers between devices, per_device(): other_half = lax.ppermute(precond, 'xh', swap)  5.42 us
    all_to_all x1, starting transfers between devices, per_device(): lax.all_to_all(turned.reshape(xl_n * xh_n, 2, tokens, width), ('xl', 'xh'...  4.29 us
    ppermute x1, starting transfers between devices, per_device(): lax.ppermute(turned[:, 0], AXES, moved(lambda xl, y, c, z, xh: (xl, z, c,...  4.17 us
    pallas_call x1, Pallas kernels, score(): pl.pallas_call(score_kernel, out_shape=jax.ShapeDtypeStruct((y_n, xl_n, 8...  2.88 us
  transfers between devices with their start and end apart: 7, of which 1 were waited for; matrix products, arithmetic and copies ran while one was open for 1% of the time, Pallas kernels for 0%

profile of v4, /device:TPU:8, one launch (start us, length us, event | category | flops | bytes accessed | tf_op | source)
XLA Modules:
  0.0 90.3 jit_solution(1749434414154242842)
XLA Ops:
  0.0 0.0 copy-start
  0.0 2.3 %shard_map.64 = bf16[2,2,2,32,320]{4,3,2,1,0:T(8,128)(2,1)} custom-call(bf16[2,64,320]{2,1,0:T(8,128)(2,1)} %bitcast.26, bf16[2,64,320]{2,1,0:T(8,128)(2,1)} %bitcast.27, bf16[2,320,320]{2,1,0:T(8,128)(2,1)} %bitcast.24, bf16[2,320,320]{2,1,0:T(8,128)(2,1)} %bitcast.25), custom_call_target="tpu_custom_call" | custom-call | flops 52428800 | bytes 2097152 | tf_op jit(solution)/shard_map/pallas_call | solution.py:52
  2.3 4.3 %all-to-all-start = ((bf16[4,2,32,320]{3,2,1,0:T(8,128)(2,1)}), bf16[4,2,32,320]{3,2,1,0:T(8,128)(2,1)S(1)}, u32[]{:S(2)}, u32[]{:S(2)}) async-start(bf16[4,2,32,320]{3,2,1,0:T(8,128)(2,1)} %bitcast.23), calls=%async_computation | async-start | bytes 393216 | tf_op jit(solution)/shard_map/all_to_all | solution.py:141
  6.6 0.0 copy-done
  6.6 5.4 %collective-permute-start.1 = (bf16[2,320,320]{2,1,0:T(8,128)(2,1)S(1)}, bf16[2,320,320]{2,1,0:T(8,128)(2,1)S(1)}, u32[]{:S(2)}, u32[]{:S(2)}) collective-permute-start(bf16[2,320,320]{2,1,0:T(8,128)(2,1)S(1)} %copy-done), channel_id=1, source_target_pairs={{0,1},{1,0},{2,3},{3,2},{4,5},{5,4},{6,7},{7,6},{8,9},{9,8},{10,11... | collective-permute-start | bytes 1228808 | tf_op jit(solution)/shard_map/ppermute | solution.py:138
  12.1 1.9 %collective-permute-start.2 = (bf16[2,320,320]{2,1,0:T(8,128)(2,1)S(1)}, bf16[2,320,320]{2,1,0:T(8,128)(2,1)S(1)}, u32[]{:S(2)}, u32[]{:S(2)}) collective-permute-start(bf16[2,320,320]{2,1,0:T(8,128)(2,1)S(1)} %copy-done), channel_id=1, source_target_pairs={{0,16},{16,0},{1,17},{17,1},{2,18},{18,2},{3,19},{19,3},{4,20},{20... | collective-permute-start | bytes 1228808 | tf_op jit(solution)/shard_map/ppermute | solution.py:150
  14.0 0.0 all-to-all-done
  14.1 4.2 %collective-permute-start = (bf16[4,32,320]{2,1,0:T(8,128)(2,1)S(1)}, bf16[4,32,320]{2,1,0:T(8,128)(2,1)S(1)}, u32[]{:S(2)}, u32[]{:S(2)}) collective-permute-start(bf16[4,32,320]{2,1,0:T(8,128)(2,1)S(1)} %get-tuple-element.6), channel_id=1, source_target_pairs={{0,0},{1,1},{2,32},{3,33},{4,64},{5,65},{6,96},{7,97},{8,128},{9,1... | collective-permute-start | bytes 245768 | tf_op jit(solution)/shard_map/ppermute | solution.py:144
  18.2 0.1 pad_add_fusion.place_ref
  18.3 1.0 %broadcast_in_dim.17 = bf16[8,4,32,320]{3,2,1,0:T(8,128)(2,1)} broadcast(bf16[4,32,320]{2,1,0:T(8,128)(2,1)S(1)} %get-tuple-element.5), dimensions={1,2,3} | broadcast | bytes 737280 | tf_op jit(solution)/shard_map/broadcast_in_dim | solution.py:145
  19.3 13.8 %all-to-all-start.1 = ((bf16[8,4,32,320]{3,2,1,0:T(8,128)(2,1)}), bf16[8,4,32,320]{3,2,1,0:T(8,128)(2,1)S(1)}, u32[]{:S(2)}, u32[]{:S(2)}) async-start(bf16[8,4,32,320]{3,2,1,0:T(8,128)(2,1)} %broadcast_in_dim.17), calls=%async_computation.1 | async-start | bytes 1572864 | tf_op jit(solution)/shard_map/all_to_all | solution.py:146
  33.1 0.0 collective-permute-done.1.tables_and_out_1_
  33.1 1.9 %collective-permute-start.3 = (bf16[2,320,320]{2,1,0:T(8,128)(2,1)S(1)}, bf16[2,320,320]{2,1,0:T(8,128)(2,1)S(1)}, u32[]{:S(2)}, u32[]{:S(2)}) collective-permute-start(bf16[2,320,320]{2,1,0:T(8,128)(2,1)S(1)} %collective-permute-done.1.tables_and_out_1_), channel_id=1, source_target_pairs={{0,16},{16,0},{1,17},{17,1},{2,18},{18,2},{3,19},{19,3},{4,20},{20... | collective-permute-start | bytes 1228808 | tf_op jit(solution)/shard_map/ppermute | solution.py:150
  35.0 0.0 collective-permute-done.rows_ref
  35.1 0.0 copy-start.2
  35.1 0.6 copy-done.2
  35.7 27.5 %all-gather = bf16[32,32,320]{2,1,0:T(8,128)(2,1)S(1)} all-gather(bf16[4,32,320]{2,1,0:T(8,128)(2,1)} %shard_map.65), channel_id=2, replica_groups=mesh['xl'=2,'y'=8,'c'=2,'z'=8,'xh'=2] {'z'}, dimensions={0}, use_global_device_ids=true | all-gather | bytes 737280 | tf_op jit(solution)/shard_map/all_gather | solution.py:147
  63.2 0.0 collective-permute-done.2.tables_and_out_2_
  63.2 0.0 collective-permute-done.3.tables_and_out_3_
  63.2 0.0 all-to-all-done.1
  63.2 2.9 %shard_map.66 = f32[8,2,8,128]{3,2,1,0:T(8,128)S(1)} custom-call(s32[2]{0:T(128)S(1)} %pad_add_fusion.place_ref, bf16[8,2,2,32,320]{4,3,2,1,0:T(8,128)(2,1)S(1)} %bitcast.21, bf16[8,2,2,32,320]{4,3,2,1,0:T(8,128)(2,1)S(1)} %bitcast.20, bf16[2,320,320]{2,1,0:T(8,128)(2,1)S(1)} %copy-done, bf16[2,320,320]{2,1,0:T(8,128)(2,1)S(1)} %collective-permute-done.1.tables_and_out_1_, ...), custom_call_target="tpu_custom_call" | custom-call | flops 838860800 | bytes 4194304 | tf_op jit(solution)/shard_map/pallas_call | solution.py:117
  66.1 0.0 copy-start.1
  66.1 0.6 copy-done.1
  66.7 0.0 copy-start.3
  66.7 10.6 %all-to-all-start.2 = ((f32[128,1,128]{2,1,0:T(1,128)}), f32[128,1,128]{2,1,0:T(1,128)S(1)}, u32[]{:S(2)}, u32[]{:S(2)}) async-start(f32[128,1,128]{2,1,0:T(1,128)} %bitcast.22), calls=%async_computation.2 | async-start | bytes 131072 | tf_op jit(solution)/shard_map/all_to_all | solution.py:153
  77.4 0.0 copy-done.3
  77.4 12.1 %all-to-all-done.2 = f32[128,1,128]{2,1,0:T(1,128)S(1)} async-done(((f32[128,1,128]{2,1,0:T(1,128)}), f32[128,1,128]{2,1,0:T(1,128)S(1)}, u32[]{:S(2)}, u32[]{:S(2)}) %all-to-all-start.2) | async-done | bytes 65568 | tf_op jit(solution)/shard_map/all_to_all | solution.py:153
  89.5 0.2 reduce_sum.9
  89.7 0.1 reshape.75
  89.8 0.6 broadcast_select_fusion
  (3 shorter events, 0.0 us)
Async XLA Ops:
  0.0 6.6 %copy-start = (bf16[2,320,320]{2,1,0:T(8,128)(2,1)S(1)}, bf16[2,320,320]{2,1,0:T(8,128)(2,1)}, u32[]{:S(2)}) copy-start(bf16[2,320,320]{2,1,0:T(8,128)(2,1)} %tables_and_out_0_.1) | copy-start | bytes 1228804
  2.3 11.7 %all-to-all-start = ((bf16[4,2,32,320]{3,2,1,0:T(8,128)(2,1)}), bf16[4,2,32,320]{3,2,1,0:T(8,128)(2,1)S(1)}, u32[]{:S(2)}, u32[]{:S(2)}) async-start(bf16[4,2,32,320]{3,2,1,0:T(8,128)(2,1)} %bitcast.23), calls=%async_computation | async-start | bytes 393216 | tf_op jit(solution)/shard_map/all_to_all | solution.py:141
  6.6 26.5 %collective-permute-start.1 = (bf16[2,320,320]{2,1,0:T(8,128)(2,1)S(1)}, bf16[2,320,320]{2,1,0:T(8,128)(2,1)S(1)}, u32[]{:S(2)}, u32[]{:S(2)}) collective-permute-start(bf16[2,320,320]{2,1,0:T(8,128)(2,1)S(1)} %copy-done), channel_id=1, source_target_pairs={{0,1},{1,0},{2,3},{3,2},{4,5},{5,4},{6,7},{7,6},{8,9},{9,8},{10,11... | collective-permute-start | bytes 1228808 | tf_op jit(solution)/shard_map/ppermute | solution.py:138
  12.1 51.1 %collective-permute-start.2 = (bf16[2,320,320]{2,1,0:T(8,128)(2,1)S(1)}, bf16[2,320,320]{2,1,0:T(8,128)(2,1)S(1)}, u32[]{:S(2)}, u32[]{:S(2)}) collective-permute-start(bf16[2,320,320]{2,1,0:T(8,128)(2,1)S(1)} %copy-done), channel_id=1, source_target_pairs={{0,16},{16,0},{1,17},{17,1},{2,18},{18,2},{3,19},{19,3},{4,20},{20... | collective-permute-start | bytes 1228808 | tf_op jit(solution)/shard_map/ppermute | solution.py:150
  14.1 21.0 %collective-permute-start = (bf16[4,32,320]{2,1,0:T(8,128)(2,1)S(1)}, bf16[4,32,320]{2,1,0:T(8,128)(2,1)S(1)}, u32[]{:S(2)}, u32[]{:S(2)}) collective-permute-start(bf16[4,32,320]{2,1,0:T(8,128)(2,1)S(1)} %get-tuple-element.6), channel_id=1, source_target_pairs={{0,0},{1,1},{2,32},{3,33},{4,64},{5,65},{6,96},{7,97},{8,128},{9,1... | collective-permute-start | bytes 245768 | tf_op jit(solution)/shard_map/ppermute | solution.py:144
  19.3 43.9 %all-to-all-start.1 = ((bf16[8,4,32,320]{3,2,1,0:T(8,128)(2,1)}), bf16[8,4,32,320]{3,2,1,0:T(8,128)(2,1)S(1)}, u32[]{:S(2)}, u32[]{:S(2)}) async-start(bf16[8,4,32,320]{3,2,1,0:T(8,128)(2,1)} %broadcast_in_dim.17), calls=%async_computation.1 | async-start | bytes 1572864 | tf_op jit(solution)/shard_map/all_to_all | solution.py:146
  33.1 30.1 %collective-permute-start.3 = (bf16[2,320,320]{2,1,0:T(8,128)(2,1)S(1)}, bf16[2,320,320]{2,1,0:T(8,128)(2,1)S(1)}, u32[]{:S(2)}, u32[]{:S(2)}) collective-permute-start(bf16[2,320,320]{2,1,0:T(8,128)(2,1)S(1)} %collective-permute-done.1.tables_and_out_1_), channel_id=1, source_target_pairs={{0,16},{16,0},{1,17},{17,1},{2,18},{18,2},{3,19},{19,3},{4,20},{20... | collective-permute-start | bytes 1228808 | tf_op jit(solution)/shard_map/ppermute | solution.py:150
  35.1 0.6 copy-start.2
  66.1 0.6 copy-start.1
  66.7 10.6 %copy-start.3 = (s32[4]{0:T(128)S(1)}, s32[4]{0:T(128)}, u32[]{:S(2)}) copy-start(s32[4]{0:T(128)} %param.11) | copy-start | bytes 52
  66.7 22.8 %all-to-all-start.2 = ((f32[128,1,128]{2,1,0:T(1,128)}), f32[128,1,128]{2,1,0:T(1,128)S(1)}, u32[]{:S(2)}, u32[]{:S(2)}) async-start(f32[128,1,128]{2,1,0:T(1,128)} %bitcast.22), calls=%async_computation.2 | async-start | bytes 131072 | tf_op jit(solution)/shard_map/all_to_all | solution.py:153

commit v5 on v4

--- a/solution.py
+++ b/solution.py
@@ -7,7 +7,6 @@
 
 AXES = ("xl", "y", "c", "z", "xh")
 SIZES = (2, 8, 2, 8, 2)
-NT = (((1,), (1,)), ((), ()))
 
 
 def moved(to):
@@ -82,32 +81,29 @@
     y_n, xl_n, _, tokens, width = act_ref.shape
     queries = table_refs[0].shape[0]
     seqs = tokens // 8
-    total = y_n * tokens
+    total = y_n * xl_n * tokens
     core, half = place_ref[0], place_ref[1]
-    lane = lax.broadcasted_iota(jnp.int32, (y_n, 8, 128), 2)
-    for xl in range(xl_n):
-        out = jnp.zeros((y_n, 8, 128), jnp.float32)
-        acts = [
-            act_ref[:, xl, core if n == 0 else 1 - core].reshape(total, width) for n in range(2)
-        ]
-        grads = [
-            grad_ref[:, xl, half if j == 0 else 1 - half].reshape(total, width).astype(jnp.float32)
-            for j in range(2)
-        ]
-        for query in range(queries):
-            running = jnp.zeros((total, width), jnp.float32)
-            for j in range(2):
-                projected = jnp.zeros((total, width), jnp.float32)
-                for n in range(2):
-                    projected += lax.dot_general(
-                        acts[n], table_refs[2 * n + j][query], NT,
-                        preferred_element_type=jnp.float32,
-                    )
-                running += projected * grads[j]
-            column = jnp.sum(running, axis=1, keepdims=True).reshape(y_n, seqs, 8, 1)
-            for seq in range(seqs):
-                out = jnp.where(lane == query * seqs + seq, column[:, seq], out)
-        out_ref[:, xl] = out
+    act = jnp.concatenate(
+        [act_ref[:, :, block].reshape(total, width) for block in (core, 1 - core)], axis=1
+    ).astype(jnp.float32)
+    grad = jnp.concatenate(
+        [grad_ref[:, :, block].reshape(total, width) for block in (half, 1 - half)], axis=1
+    )
+    lane = lax.broadcasted_iota(jnp.int32, (y_n, xl_n, 8, 128), 3)
+    out = jnp.zeros((y_n, xl_n, 8, 128), jnp.float32)
+    for query in range(queries):
+        table = jnp.concatenate(
+            [
+                jnp.concatenate([table_refs[j][query], table_refs[2 + j][query]], axis=1)
+                for j in range(2)
+            ]
+        )
+        projected = jnp.dot(grad, table, preferred_element_type=jnp.float32)
+        column = jnp.sum(projected * act, axis=1, keepdims=True)
+        column = column.reshape(y_n, xl_n, seqs, 8, 1)
+        for seq in range(seqs):
+            out = jnp.where(lane == query * seqs + seq, column[:, :, seq], out)
+    out_ref[...] = out
 
 
 def score(place, act, grad, tables):

time: 90.8 us -> 89.9 us (0.990)
  no operation moved by 1% of the time
where the time goes in v5:
time: 89.9 us; the launch traced here: 89.5 us
  starting transfers between devices  42.2 us (47%)
  blocking collectives  27.5 us (31%)
  waiting for transfers between devices  12.1 us (13%)
  Pallas kernels  4.38 us (5%)
  local copies, waits for them, and re-layouts  2.35 us (3%)
    all_gather x1, blocking collectives, per_device(): act = lax.all_gather(hold(act), 'z', axis=0, tiled=False)  27.5 us
    all_to_all x1, starting transfers between devices, per_device(): grad = lax.all_to_all(grad, 'y', 0, 0, tiled=True)  13.8 us
    all_to_all x1, waiting for transfers between devices, per_device(): lax.all_to_all(partial_scores.reshape(y_n * xl_n * z_n, 1, 128), ('y', 'x...  12.1 us
    all_to_all x1, starting transfers between devices, per_device(): lax.all_to_all(partial_scores.reshape(y_n * xl_n * z_n, 1, 128), ('y', 'x...  10.6 us
    ppermute x1, starting transfers between devices, per_device(): other_half = lax.ppermute(precond, 'xh', swap)  5.42 us
    all_to_all x1, starting transfers between devices, per_device(): lax.all_to_all(turned.reshape(xl_n * xh_n, 2, tokens, width), ('xl', 'xh'...  4.29 us
    ppermute x1, starting transfers between devices, per_device(): lax.ppermute(turned[:, 0], AXES, moved(lambda xl, y, c, z, xh: (xl, z, c,...  4.17 us
    pallas_call x1, Pallas kernels, rotate(): pl.pallas_call(rotate_kernel, out_shape=jax.ShapeDtypeStruct((layers, 2,...  2.33 us
  transfers between devices with their start and end apart: 7, of which 1 were waited for; matrix products, arithmetic and copies ran while one was open for 1% of the time, Pallas kernels for 0%

profile of v5, /device:TPU:8, one launch (start us, length us, event | category | flops | bytes accessed | tf_op | source)
XLA Modules:
  0.0 89.5 jit_solution(6818007455240645825)
XLA Ops:
  0.0 0.0 copy-start
  0.0 2.3 %shard_map.64 = bf16[2,2,2,32,320]{4,3,2,1,0:T(8,128)(2,1)} custom-call(bf16[2,64,320]{2,1,0:T(8,128)(2,1)} %bitcast.26, bf16[2,64,320]{2,1,0:T(8,128)(2,1)} %bitcast.27, bf16[2,320,320]{2,1,0:T(8,128)(2,1)} %bitcast.24, bf16[2,320,320]{2,1,0:T(8,128)(2,1)} %bitcast.25), custom_call_target="tpu_custom_call" | custom-call | flops 52428800 | bytes 2097152 | tf_op jit(solution)/shard_map/pallas_call | solution.py:51
  2.3 4.3 %all-to-all-start = ((bf16[4,2,32,320]{3,2,1,0:T(8,128)(2,1)}), bf16[4,2,32,320]{3,2,1,0:T(8,128)(2,1)S(1)}, u32[]{:S(2)}, u32[]{:S(2)}) async-start(bf16[4,2,32,320]{3,2,1,0:T(8,128)(2,1)} %bitcast.23), calls=%async_computation | async-start | bytes 393216 | tf_op jit(solution)/shard_map/all_to_all | solution.py:137
  6.6 0.0 copy-done
  6.6 5.4 %collective-permute-start.1 = (bf16[2,320,320]{2,1,0:T(8,128)(2,1)S(1)}, bf16[2,320,320]{2,1,0:T(8,128)(2,1)S(1)}, u32[]{:S(2)}, u32[]{:S(2)}) collective-permute-start(bf16[2,320,320]{2,1,0:T(8,128)(2,1)S(1)} %copy-done), channel_id=1, source_target_pairs={{0,1},{1,0},{2,3},{3,2},{4,5},{5,4},{6,7},{7,6},{8,9},{9,8},{10,11... | collective-permute-start | bytes 1228808 | tf_op jit(solution)/shard_map/ppermute | solution.py:134
  12.1 1.9 %collective-permute-start.2 = (bf16[2,320,320]{2,1,0:T(8,128)(2,1)S(1)}, bf16[2,320,320]{2,1,0:T(8,128)(2,1)S(1)}, u32[]{:S(2)}, u32[]{:S(2)}) collective-permute-start(bf16[2,320,320]{2,1,0:T(8,128)(2,1)S(1)} %copy-done), channel_id=1, source_target_pairs={{0,16},{16,0},{1,17},{17,1},{2,18},{18,2},{3,19},{19,3},{4,20},{20... | collective-permute-start | bytes 1228808 | tf_op jit(solution)/shard_map/ppermute | solution.py:146
  14.0 0.0 all-to-all-done
  14.1 4.2 %collective-permute-start = (bf16[4,32,320]{2,1,0:T(8,128)(2,1)S(1)}, bf16[4,32,320]{2,1,0:T(8,128)(2,1)S(1)}, u32[]{:S(2)}, u32[]{:S(2)}) collective-permute-start(bf16[4,32,320]{2,1,0:T(8,128)(2,1)S(1)} %get-tuple-element.6), channel_id=1, source_target_pairs={{0,0},{1,1},{2,32},{3,33},{4,64},{5,65},{6,96},{7,97},{8,128},{9,1... | collective-permute-start | bytes 245768 | tf_op jit(solution)/shard_map/ppermute | solution.py:140
  18.2 0.1 pad_add_fusion.place_ref
  18.3 1.0 %broadcast_in_dim.17 = bf16[8,4,32,320]{3,2,1,0:T(8,128)(2,1)} broadcast(bf16[4,32,320]{2,1,0:T(8,128)(2,1)S(1)} %get-tuple-element.5), dimensions={1,2,3} | broadcast | bytes 737280 | tf_op jit(solution)/shard_map/broadcast_in_dim | solution.py:141
  19.3 13.8 %all-to-all-start.1 = ((bf16[8,4,32,320]{3,2,1,0:T(8,128)(2,1)}), bf16[8,4,32,320]{3,2,1,0:T(8,128)(2,1)S(1)}, u32[]{:S(2)}, u32[]{:S(2)}) async-start(bf16[8,4,32,320]{3,2,1,0:T(8,128)(2,1)} %broadcast_in_dim.17), calls=%async_computation.1 | async-start | bytes 1572864 | tf_op jit(solution)/shard_map/all_to_all | solution.py:142
  33.1 0.0 collective-permute-done.1.tables_and_out_1_
  33.1 1.9 %collective-permute-start.3 = (bf16[2,320,320]{2,1,0:T(8,128)(2,1)S(1)}, bf16[2,320,320]{2,1,0:T(8,128)(2,1)S(1)}, u32[]{:S(2)}, u32[]{:S(2)}) collective-permute-start(bf16[2,320,320]{2,1,0:T(8,128)(2,1)S(1)} %collective-permute-done.1.tables_and_out_1_), channel_id=1, source_target_pairs={{0,16},{16,0},{1,17},{17,1},{2,18},{18,2},{3,19},{19,3},{4,20},{20... | collective-permute-start | bytes 1228808 | tf_op jit(solution)/shard_map/ppermute | solution.py:146
  35.0 0.0 collective-permute-done.rows_ref
  35.1 0.0 copy-start.2
  35.1 0.6 copy-done.2
  35.7 27.5 %all-gather = bf16[32,32,320]{2,1,0:T(8,128)(2,1)S(1)} all-gather(bf16[4,32,320]{2,1,0:T(8,128)(2,1)} %shard_map.65), channel_id=2, replica_groups=mesh['xl'=2,'y'=8,'c'=2,'z'=8,'xh'=2] {'z'}, dimensions={0}, use_global_device_ids=true | all-gather | bytes 737280 | tf_op jit(solution)/shard_map/all_gather | solution.py:143
  63.2 0.0 collective-permute-done.2.tables_and_out_2_
  63.2 0.0 collective-permute-done.3.tables_and_out_3_
  63.2 0.0 all-to-all-done.1
  63.2 2.0 %shard_map.66 = f32[8,2,8,128]{3,2,1,0:T(8,128)S(1)} custom-call(s32[2]{0:T(128)S(1)} %pad_add_fusion.place_ref, bf16[8,2,2,32,320]{4,3,2,1,0:T(8,128)(2,1)S(1)} %bitcast.21, bf16[8,2,2,32,320]{4,3,2,1,0:T(8,128)(2,1)S(1)} %bitcast.20, bf16[2,320,320]{2,1,0:T(8,128)(2,1)S(1)} %copy-done, bf16[2,320,320]{2,1,0:T(8,128)(2,1)S(1)} %collective-permute-done.1.tables_and_out_1_, ...), custom_call_target="tpu_custom_call" | custom-call | flops 838860800 | bytes 4194304 | tf_op jit(solution)/shard_map/pallas_call | solution.py:113
  65.3 0.0 copy-start.1
  65.3 0.6 copy-done.1
  65.9 0.0 copy-start.3
  65.9 10.6 %all-to-all-start.2 = ((f32[128,1,128]{2,1,0:T(1,128)}), f32[128,1,128]{2,1,0:T(1,128)S(1)}, u32[]{:S(2)}, u32[]{:S(2)}) async-start(f32[128,1,128]{2,1,0:T(1,128)} %bitcast.22), calls=%async_computation.2 | async-start | bytes 131072 | tf_op jit(solution)/shard_map/all_to_all | solution.py:149
  76.5 0.0 copy-done.3
  76.6 12.1 %all-to-all-done.2 = f32[128,1,128]{2,1,0:T(1,128)S(1)} async-done(((f32[128,1,128]{2,1,0:T(1,128)}), f32[128,1,128]{2,1,0:T(1,128)S(1)}, u32[]{:S(2)}, u32[]{:S(2)}) %all-to-all-start.2) | async-done | bytes 65568 | tf_op jit(solution)/shard_map/all_to_all | solution.py:149
  88.7 0.2 reduce_sum.9
  88.9 0.1 reshape.75
  88.9 0.6 broadcast_select_fusion
  (3 shorter events, 0.0 us)
Async XLA Ops:
  0.0 6.6 %copy-start = (bf16[2,320,320]{2,1,0:T(8,128)(2,1)S(1)}, bf16[2,320,320]{2,1,0:T(8,128)(2,1)}, u32[]{:S(2)}) copy-start(bf16[2,320,320]{2,1,0:T(8,128)(2,1)} %tables_and_out_0_.1) | copy-start | bytes 1228804
  2.3 11.7 %all-to-all-start = ((bf16[4,2,32,320]{3,2,1,0:T(8,128)(2,1)}), bf16[4,2,32,320]{3,2,1,0:T(8,128)(2,1)S(1)}, u32[]{:S(2)}, u32[]{:S(2)}) async-start(bf16[4,2,32,320]{3,2,1,0:T(8,128)(2,1)} %bitcast.23), calls=%async_computation | async-start | bytes 393216 | tf_op jit(solution)/shard_map/all_to_all | solution.py:137
  6.6 26.5 %collective-permute-start.1 = (bf16[2,320,320]{2,1,0:T(8,128)(2,1)S(1)}, bf16[2,320,320]{2,1,0:T(8,128)(2,1)S(1)}, u32[]{:S(2)}, u32[]{:S(2)}) collective-permute-start(bf16[2,320,320]{2,1,0:T(8,128)(2,1)S(1)} %copy-done), channel_id=1, source_target_pairs={{0,1},{1,0},{2,3},{3,2},{4,5},{5,4},{6,7},{7,6},{8,9},{9,8},{10,11... | collective-permute-start | bytes 1228808 | tf_op jit(solution)/shard_map/ppermute | solution.py:134
  12.1 51.1 %collective-permute-start.2 = (bf16[2,320,320]{2,1,0:T(8,128)(2,1)S(1)}, bf16[2,320,320]{2,1,0:T(8,128)(2,1)S(1)}, u32[]{:S(2)}, u32[]{:S(2)}) collective-permute-start(bf16[2,320,320]{2,1,0:T(8,128)(2,1)S(1)} %copy-done), channel_id=1, source_target_pairs={{0,16},{16,0},{1,17},{17,1},{2,18},{18,2},{3,19},{19,3},{4,20},{20... | collective-permute-start | bytes 1228808 | tf_op jit(solution)/shard_map/ppermute | solution.py:146
  14.1 21.0 %collective-permute-start = (bf16[4,32,320]{2,1,0:T(8,128)(2,1)S(1)}, bf16[4,32,320]{2,1,0:T(8,128)(2,1)S(1)}, u32[]{:S(2)}, u32[]{:S(2)}) collective-permute-start(bf16[4,32,320]{2,1,0:T(8,128)(2,1)S(1)} %get-tuple-element.6), channel_id=1, source_target_pairs={{0,0},{1,1},{2,32},{3,33},{4,64},{5,65},{6,96},{7,97},{8,128},{9,1... | collective-permute-start | bytes 245768 | tf_op jit(solution)/shard_map/ppermute | solution.py:140
  19.3 43.9 %all-to-all-start.1 = ((bf16[8,4,32,320]{3,2,1,0:T(8,128)(2,1)}), bf16[8,4,32,320]{3,2,1,0:T(8,128)(2,1)S(1)}, u32[]{:S(2)}, u32[]{:S(2)}) async-start(bf16[8,4,32,320]{3,2,1,0:T(8,128)(2,1)} %broadcast_in_dim.17), calls=%async_computation.1 | async-start | bytes 1572864 | tf_op jit(solution)/shard_map/all_to_all | solution.py:142
  33.1 30.1 %collective-permute-start.3 = (bf16[2,320,320]{2,1,0:T(8,128)(2,1)S(1)}, bf16[2,320,320]{2,1,0:T(8,128)(2,1)S(1)}, u32[]{:S(2)}, u32[]{:S(2)}) collective-permute-start(bf16[2,320,320]{2,1,0:T(8,128)(2,1)S(1)} %collective-permute-done.1.tables_and_out_1_), channel_id=1, source_target_pairs={{0,16},{16,0},{1,17},{17,1},{2,18},{18,2},{3,19},{19,3},{4,20},{20... | collective-permute-start | bytes 1228808 | tf_op jit(solution)/shard_map/ppermute | solution.py:146
  35.1 0.6 copy-start.2
  65.3 0.6 copy-start.1
  65.9 10.6 %copy-start.3 = (s32[4]{0:T(128)S(1)}, s32[4]{0:T(128)}, u32[]{:S(2)}) copy-start(s32[4]{0:T(128)} %param.11) | copy-start | bytes 52
  65.9 22.8 %all-to-all-start.2 = ((f32[128,1,128]{2,1,0:T(1,128)}), f32[128,1,128]{2,1,0:T(1,128)S(1)}, u32[]{:S(2)}, u32[]{:S(2)}) async-start(f32[128,1,128]{2,1,0:T(1,128)} %bitcast.22), calls=%async_computation.2 | async-start | bytes 131072 | tf_op jit(solution)/shard_map/all_to_all | solution.py:149

commit v6 on v5

--- a/solution.py
+++ b/solution.py
@@ -82,9 +82,14 @@
     queries = table_refs[0].shape[0]
     seqs = tokens // 8
     total = y_n * xl_n * tokens
-    core, half = place_ref[0], place_ref[1]
+    core, half, row = place_ref[0], place_ref[1], place_ref[2]
+    places = [lax.rem(2 * row + y_n + y_n // 2 - y, y_n) for y in range(y_n)]
     act = jnp.concatenate(
-        [act_ref[:, :, block].reshape(total, width) for block in (core, 1 - core)], axis=1
+        [
+            jnp.concatenate([act_ref[place, :, block] for place in places]).reshape(total, width)
+            for block in (core, 1 - core)
+        ],
+        axis=1,
     ).astype(jnp.float32)
     grad = jnp.concatenate(
         [grad_ref[:, :, block].reshape(total, width) for block in (half, 1 - half)], axis=1
@@ -103,7 +108,12 @@
         column = column.reshape(y_n, xl_n, seqs, 8, 1)
         for seq in range(seqs):
             out = jnp.where(lane == query * seqs + seq, column[:, :, seq], out)
-    out_ref[...] = out
+    length = jnp.full(out.shape, place_ref[3])
+    for seq in range(1, seqs):
+        length = jnp.where(lax.rem(lane, seqs) == seq, place_ref[3 + seq], length)
+    y, xl, z = (lax.broadcasted_iota(jnp.int32, out.shape, axis) for axis in range(3))
+    position = ((xl * y_n + y) * 2 + core) * 16 + z * 2 + half
+    out_ref[...] = jnp.where(position < length, out, 0.0)
 
 
 def score(place, act, grad, tables):
@@ -130,14 +140,18 @@
     queries = precond.shape[0]
     tokens = seqs * span // 2
     swap = [(0, 1), (1, 0)]
-    place = jnp.stack([lax.axis_index("c"), lax.axis_index("xh")]).astype(jnp.int32)
+    place = jnp.stack([lax.axis_index(axis) for axis in ("c", "xh", "y")]).astype(jnp.int32)
+    place = jnp.concatenate([place, lengths])
     other_half = lax.ppermute(precond, "xh", swap)
 
     turned = rotate(act_rows, grad_rows, eig_act, eig_grad)
     turned = lax.all_to_all(
         turned.reshape(xl_n * xh_n, 2, tokens, width), ("xl", "xh"), 0, 0, tiled=True
     )
-    act = lax.ppermute(turned[:, 0], AXES, moved(lambda xl, y, c, z, xh: (xl, z, c, y, xh)))
+    act = lax.ppermute(
+        turned[:, 0], AXES,
+        moved(lambda xl, y, c, z, xh: (xl, z, c, (2 * z + z_n // 2 - y) % z_n, xh)),
+    )
     grad = jnp.broadcast_to(turned[:, 1], (y_n, xl_n * xh_n, tokens, width))
     grad = lax.all_to_all(grad, "y", 0, 0, tiled=True)
     act = lax.all_gather(hold(act), "z", axis=0, tiled=False)
@@ -149,10 +163,7 @@
     shares = lax.all_to_all(
         partial_scores.reshape(y_n * xl_n * z_n, 1, 128), ("y", "xl", "z"), 0, 0, tiled=True
     )
-    summed = jnp.sum(shares, axis=(0, 1))[: queries * seqs].reshape(queries, seqs, 1)
-    position = lax.axis_index(AXES)
-    valid_mask = position < lengths
-    return jnp.where(valid_mask[None, :, None], summed, 0.0)
+    return jnp.sum(shares, axis=(0, 1))[: queries * seqs].reshape(queries, seqs, 1)
 
 
 def solution(mesh):

time: 89.9 us -> 89.7 us (level)
  blocking collectives: 27.5 us -> 50.9 us
  waiting for transfers between devices: 12.1 us -> 0.02 us
  starting transfers between devices: 42.2 us -> 30.7 us
    all_to_all x0 -> x1, blocking collectives: none -> 24.6 us  [per_device(): lax.all_to_all(partial_scores.reshape(y_n * xl_n * z_n, 1, 128), ('y', 'x...]
    all_to_all x1 -> x0, waiting for transfers between devices: 12.1 us -> none  [per_device(): lax.all_to_all(partial_scores.reshape(y_n * xl_n * z_n, 1, 128), ('y', 'x...]
    all_to_all x1 -> x0, starting transfers between devices: 10.6 us -> none  [per_device(): lax.all_to_all(partial_scores.reshape(y_n * xl_n * z_n, 1, 128), ('y', 'x...]
    all_to_all x1, starting transfers between devices: 13.8 us -> 9.36 us  [per_device(): grad = lax.all_to_all(grad, 'y', 0, 0, tiled=True)]
    ppermute x1, starting transfers between devices: 4.17 us -> 7.78 us  [per_device(): lax.ppermute(turned[:, 0], AXES, moved(lambda xl, y, c, z, xh: (xl, z, c,...]
    all_gather x1, blocking collectives: 27.5 us -> 26.3 us  [per_device(): act = lax.all_gather(hold(act), 'z', axis=0, tiled=False)]
  transfers between devices with their start and end apart: 7 -> 6, of which waited for: 1 -> 0; matrix products, arithmetic and copies ran while one was open for 1% -> 1% of each run, Pallas kernels for 0% -> 0%
where the time goes in v6:
time: 89.7 us; the launch traced here: 89.2 us
  blocking collectives  50.9 us (57%)
  starting transfers between devices  30.7 us (34%)
  Pallas kernels  4.37 us (5%)
  local copies, waits for them, and re-layouts  2.94 us (3%)
    all_gather x1, blocking collectives, per_device(): act = lax.all_gather(hold(act), 'z', axis=0, tiled=False)  26.3 us
    all_to_all x1, blocking collectives, per_device(): lax.all_to_all(partial_scores.reshape(y_n * xl_n * z_n, 1, 128), ('y', 'x...  24.6 us
    all_to_all x1, starting transfers between devices, per_device(): grad = lax.all_to_all(grad, 'y', 0, 0, tiled=True)  9.36 us
    ppermute x1, starting transfers between devices, per_device(): lax.ppermute(turned[:, 0], AXES, moved(lambda xl, y, c, z, xh: (xl, z, c,...  7.78 us
    ppermute x1, starting transfers between devices, per_device(): other_half = lax.ppermute(precond, 'xh', swap)  5.42 us
    all_to_all x1, starting transfers between devices, per_device(): lax.all_to_all(turned.reshape(xl_n * xh_n, 2, tokens, width), ('xl', 'xh'...  4.29 us
    pallas_call x1, Pallas kernels, rotate(): pl.pallas_call(rotate_kernel, out_shape=jax.ShapeDtypeStruct((layers, 2,...  2.33 us
    pallas_call x1, Pallas kernels, score(): pl.pallas_call(score_kernel, out_shape=jax.ShapeDtypeStruct((y_n, xl_n, 8...  2.04 us
  transfers between devices with their start and end apart: 6, of which 0 were waited for; matrix products, arithmetic and copies ran while one was open for 1% of the time, Pallas kernels for 0%

profile of v6, /device:TPU:8, one launch (start us, length us, event | category | flops | bytes accessed | tf_op | source)
XLA Modules:
  0.0 89.2 jit_solution(1370499110196762080)
XLA Ops:
  0.0 0.0 copy-start
  0.0 2.3 %shard_map.64 = bf16[2,2,2,32,320]{4,3,2,1,0:T(8,128)(2,1)} custom-call(bf16[2,64,320]{2,1,0:T(8,128)(2,1)} %bitcast.27, bf16[2,64,320]{2,1,0:T(8,128)(2,1)} %bitcast.28, bf16[2,320,320]{2,1,0:T(8,128)(2,1)} %bitcast.25, bf16[2,320,320]{2,1,0:T(8,128)(2,1)} %bitcast.26), custom_call_target="tpu_custom_call" | custom-call | flops 52428800 | bytes 2097152 | tf_op jit(solution)/shard_map/pallas_call | solution.py:51
  2.3 4.3 %all-to-all-start = ((bf16[4,2,32,320]{3,2,1,0:T(8,128)(2,1)}), bf16[4,2,32,320]{3,2,1,0:T(8,128)(2,1)S(1)}, u32[]{:S(2)}, u32[]{:S(2)}) async-start(bf16[4,2,32,320]{3,2,1,0:T(8,128)(2,1)} %bitcast.24), calls=%async_computation | async-start | bytes 393216 | tf_op jit(solution)/shard_map/all_to_all | solution.py:148
  6.6 0.0 copy-done
  6.6 5.4 %collective-permute-start.1 = (bf16[2,320,320]{2,1,0:T(8,128)(2,1)S(1)}, bf16[2,320,320]{2,1,0:T(8,128)(2,1)S(1)}, u32[]{:S(2)}, u32[]{:S(2)}) collective-permute-start(bf16[2,320,320]{2,1,0:T(8,128)(2,1)S(1)} %copy-done), channel_id=1, source_target_pairs={{0,1},{1,0},{2,3},{3,2},{4,5},{5,4},{6,7},{7,6},{8,9},{9,8},{10,11... | collective-permute-start | bytes 1228808 | tf_op jit(solution)/shard_map/ppermute | solution.py:145
  12.1 1.9 %collective-permute-start.2 = (bf16[2,320,320]{2,1,0:T(8,128)(2,1)S(1)}, bf16[2,320,320]{2,1,0:T(8,128)(2,1)S(1)}, u32[]{:S(2)}, u32[]{:S(2)}) collective-permute-start(bf16[2,320,320]{2,1,0:T(8,128)(2,1)S(1)} %copy-done), channel_id=1, source_target_pairs={{0,16},{16,0},{1,17},{17,1},{2,18},{18,2},{3,19},{19,3},{4,20},{20... | collective-permute-start | bytes 1228808 | tf_op jit(solution)/shard_map/ppermute | solution.py:160
  14.0 0.0 all-to-all-done
  14.0 7.8 %collective-permute-start = (bf16[4,32,320]{2,1,0:T(8,128)(2,1)S(1)}, bf16[4,32,320]{2,1,0:T(8,128)(2,1)S(1)}, u32[]{:S(2)}, u32[]{:S(2)}) collective-permute-start(bf16[4,32,320]{2,1,0:T(8,128)(2,1)S(1)} %get-tuple-element.6), channel_id=1, source_target_pairs={{0,8},{1,9},{2,44},{3,45},{4,64},{5,65},{6,100},{7,101},{8,136},{9... | collective-permute-start | bytes 245768 | tf_op jit(solution)/shard_map/ppermute | solution.py:151
  21.8 0.0 copy-start.2
  21.8 0.6 copy-done.2
  22.5 0.1 pad_add_fusion.place_ref
  22.6 1.0 %broadcast_in_dim.3 = bf16[8,4,32,320]{3,2,1,0:T(8,128)(2,1)} broadcast(bf16[4,32,320]{2,1,0:T(8,128)(2,1)S(1)} %get-tuple-element.5), dimensions={1,2,3} | broadcast | bytes 737280 | tf_op jit(solution)/shard_map/broadcast_in_dim | solution.py:155
  23.5 9.4 %all-to-all-start.1 = ((bf16[8,4,32,320]{3,2,1,0:T(8,128)(2,1)}), bf16[8,4,32,320]{3,2,1,0:T(8,128)(2,1)S(1)}, u32[]{:S(2)}, u32[]{:S(2)}) async-start(bf16[8,4,32,320]{3,2,1,0:T(8,128)(2,1)} %broadcast_in_dim.3), calls=%async_computation.1 | async-start | bytes 1572864 | tf_op jit(solution)/shard_map/all_to_all | solution.py:156
  32.9 0.0 collective-permute-done.1.tables_and_out_1_
  32.9 1.9 %collective-permute-start.3 = (bf16[2,320,320]{2,1,0:T(8,128)(2,1)S(1)}, bf16[2,320,320]{2,1,0:T(8,128)(2,1)S(1)}, u32[]{:S(2)}, u32[]{:S(2)}) collective-permute-start(bf16[2,320,320]{2,1,0:T(8,128)(2,1)S(1)} %collective-permute-done.1.tables_and_out_1_), channel_id=1, source_target_pairs={{0,16},{16,0},{1,17},{17,1},{2,18},{18,2},{3,19},{19,3},{4,20},{20... | collective-permute-start | bytes 1228808 | tf_op jit(solution)/shard_map/ppermute | solution.py:160
  34.8 0.0 collective-permute-done.rows_ref
  34.8 0.0 copy-start.1
  34.8 0.6 copy-done.1
  35.5 26.3 %all-gather = bf16[32,32,320]{2,1,0:T(8,128)(2,1)S(1)} all-gather(bf16[4,32,320]{2,1,0:T(8,128)(2,1)} %shard_map.65), channel_id=2, replica_groups=mesh['xl'=2,'y'=8,'c'=2,'z'=8,'xh'=2] {'z'}, dimensions={0}, use_global_device_ids=true | all-gather | bytes 737280 | tf_op jit(solution)/shard_map/all_gather | solution.py:157
  61.8 0.0 collective-permute-done.2.tables_and_out_2_
  61.8 0.0 collective-permute-done.3.tables_and_out_3_
  61.8 0.0 all-to-all-done.1
  61.8 2.0 %shard_map.66 = f32[8,2,8,128]{3,2,1,0:T(8,128)S(1)} custom-call(s32[7]{0:T(128)S(1)} %pad_add_fusion.place_ref, bf16[8,2,2,32,320]{4,3,2,1,0:T(8,128)(2,1)S(1)} %bitcast.22, bf16[8,2,2,32,320]{4,3,2,1,0:T(8,128)(2,1)S(1)} %bitcast.21, bf16[2,320,320]{2,1,0:T(8,128)(2,1)S(1)} %copy-done, bf16[2,320,320]{2,1,0:T(8,128)(2,1)S(1)} %collective-permute-done.1.tables_and_out_1_, ...), custom_call_target="tpu_custom_call" | custom-call | flops 838860800 | bytes 4194304 | tf_op jit(solution)/shard_map/pallas_call | solution.py:123
  63.9 24.6 %all_to_all.15 = f32[128,1,128]{2,1,0:T(1,128)S(1)} all-to-all(f32[128,1,128]{2,1,0:T(1,128)S(1)} %bitcast.23), channel_id=1, replica_groups=mesh['xl'=2,'y'=8,'c'=2,'z'=8,'xh'=2] {'y','xl','z'}, dimensions={0} | all-to-all | bytes 131072 | tf_op jit(solution)/shard_map/all_to_all | solution.py:163
  88.4 0.2 reduce_sum.9
  88.6 0.6 reshape.43
  (2 shorter events, 0.0 us)
Async XLA Ops:
  0.0 6.6 %copy-start = (bf16[2,320,320]{2,1,0:T(8,128)(2,1)S(1)}, bf16[2,320,320]{2,1,0:T(8,128)(2,1)}, u32[]{:S(2)}) copy-start(bf16[2,320,320]{2,1,0:T(8,128)(2,1)} %tables_and_out_0_.1) | copy-start | bytes 1228804
  2.3 11.7 %all-to-all-start = ((bf16[4,2,32,320]{3,2,1,0:T(8,128)(2,1)}), bf16[4,2,32,320]{3,2,1,0:T(8,128)(2,1)S(1)}, u32[]{:S(2)}, u32[]{:S(2)}) async-start(bf16[4,2,32,320]{3,2,1,0:T(8,128)(2,1)} %bitcast.24), calls=%async_computation | async-start | bytes 393216 | tf_op jit(solution)/shard_map/all_to_all | solution.py:148
  6.6 26.3 %collective-permute-start.1 = (bf16[2,320,320]{2,1,0:T(8,128)(2,1)S(1)}, bf16[2,320,320]{2,1,0:T(8,128)(2,1)S(1)}, u32[]{:S(2)}, u32[]{:S(2)}) collective-permute-start(bf16[2,320,320]{2,1,0:T(8,128)(2,1)S(1)} %copy-done), channel_id=1, source_target_pairs={{0,1},{1,0},{2,3},{3,2},{4,5},{5,4},{6,7},{7,6},{8,9},{9,8},{10,11... | collective-permute-start | bytes 1228808 | tf_op jit(solution)/shard_map/ppermute | solution.py:145
  12.1 49.7 %collective-permute-start.2 = (bf16[2,320,320]{2,1,0:T(8,128)(2,1)S(1)}, bf16[2,320,320]{2,1,0:T(8,128)(2,1)S(1)}, u32[]{:S(2)}, u32[]{:S(2)}) collective-permute-start(bf16[2,320,320]{2,1,0:T(8,128)(2,1)S(1)} %copy-done), channel_id=1, source_target_pairs={{0,16},{16,0},{1,17},{17,1},{2,18},{18,2},{3,19},{19,3},{4,20},{20... | collective-permute-start | bytes 1228808 | tf_op jit(solution)/shard_map/ppermute | solution.py:160
  14.0 20.8 %collective-permute-start = (bf16[4,32,320]{2,1,0:T(8,128)(2,1)S(1)}, bf16[4,32,320]{2,1,0:T(8,128)(2,1)S(1)}, u32[]{:S(2)}, u32[]{:S(2)}) collective-permute-start(bf16[4,32,320]{2,1,0:T(8,128)(2,1)S(1)} %get-tuple-element.6), channel_id=1, source_target_pairs={{0,8},{1,9},{2,44},{3,45},{4,64},{5,65},{6,100},{7,101},{8,136},{9... | collective-permute-start | bytes 245768 | tf_op jit(solution)/shard_map/ppermute | solution.py:151
  21.8 0.7 copy-start.2
  23.5 38.3 %all-to-all-start.1 = ((bf16[8,4,32,320]{3,2,1,0:T(8,128)(2,1)}), bf16[8,4,32,320]{3,2,1,0:T(8,128)(2,1)S(1)}, u32[]{:S(2)}, u32[]{:S(2)}) async-start(bf16[8,4,32,320]{3,2,1,0:T(8,128)(2,1)} %broadcast_in_dim.3), calls=%async_computation.1 | async-start | bytes 1572864 | tf_op jit(solution)/shard_map/all_to_all | solution.py:156
  32.9 28.9 %collective-permute-start.3 = (bf16[2,320,320]{2,1,0:T(8,128)(2,1)S(1)}, bf16[2,320,320]{2,1,0:T(8,128)(2,1)S(1)}, u32[]{:S(2)}, u32[]{:S(2)}) collective-permute-start(bf16[2,320,320]{2,1,0:T(8,128)(2,1)S(1)} %collective-permute-done.1.tables_and_out_1_), channel_id=1, source_target_pairs={{0,16},{16,0},{1,17},{17,1},{2,18},{18,2},{3,19},{19,3},{4,20},{20... | collective-permute-start | bytes 1228808 | tf_op jit(solution)/shard_map/ppermute | solution.py:160
  34.8 0.7 copy-start.1

commit v7 on v5

--- a/solution.py
+++ b/solution.py
@@ -103,7 +103,12 @@
         column = column.reshape(y_n, xl_n, seqs, 8, 1)
         for seq in range(seqs):
             out = jnp.where(lane == query * seqs + seq, column[:, :, seq], out)
-    out_ref[...] = out
+    length = jnp.full(out.shape, place_ref[2])
+    for seq in range(1, seqs):
+        length = jnp.where(lax.rem(lane, seqs) == seq, place_ref[2 + seq], length)
+    y, xl, z = (lax.broadcasted_iota(jnp.int32, out.shape, axis) for axis in range(3))
+    position = ((xl * y_n + y) * 2 + core) * 16 + z * 2 + half
+    out_ref[...] = jnp.where(position < length, out, 0.0)
 
 
 def score(place, act, grad, tables):
@@ -131,6 +136,7 @@
     tokens = seqs * span // 2
     swap = [(0, 1), (1, 0)]
     place = jnp.stack([lax.axis_index("c"), lax.axis_index("xh")]).astype(jnp.int32)
+    place = jnp.concatenate([place, lengths])
     other_half = lax.ppermute(precond, "xh", swap)
 
     turned = rotate(act_rows, grad_rows, eig_act, eig_grad)
@@ -149,10 +155,7 @@
     shares = lax.all_to_all(
         partial_scores.reshape(y_n * xl_n * z_n, 1, 128), ("y", "xl", "z"), 0, 0, tiled=True
     )
-    summed = jnp.sum(shares, axis=(0, 1))[: queries * seqs].reshape(queries, seqs, 1)
-    position = lax.axis_index(AXES)
-    valid_mask = position < lengths
-    return jnp.where(valid_mask[None, :, None], summed, 0.0)
+    return jnp.sum(shares, axis=(0, 1))[: queries * seqs].reshape(queries, seqs, 1)
 
 
 def solution(mesh):

time: 89.9 us -> 89.6 us (level)
  blocking collectives: 27.5 us -> 50 us
  waiting for transfers between devices: 12.1 us -> 0.02 us
  starting transfers between devices: 42.2 us -> 31.6 us
    all_to_all x0 -> x1, blocking collectives: none -> 23 us  [per_device(): lax.all_to_all(partial_scores.reshape(y_n * xl_n * z_n, 1, 128), ('y', 'x...]
    all_to_all x1 -> x0, waiting for transfers between devices: 12.1 us -> none  [per_device(): lax.all_to_all(partial_scores.reshape(y_n * xl_n * z_n, 1, 128), ('y', 'x...]
    all_to_all x1 -> x0, starting transfers between devices: 10.6 us -> none  [per_device(): lax.all_to_all(partial_scores.reshape(y_n * xl_n * z_n, 1, 128), ('y', 'x...]
  transfers between devices with their start and end apart: 7 -> 6, of which waited for: 1 -> 0; matrix products, arithmetic and copies ran while one was open for 1% -> 1% of each run, Pallas kernels for 0% -> 0%
where the time goes in v7:
time: 89.6 us; the launch traced here: 89.2 us
  blocking collectives  50 us (56%)
  starting transfers between devices  31.6 us (35%)
  Pallas kernels  4.37 us (5%)
  local copies, waits for them, and re-layouts  2.94 us (3%)
    all_gather x1, blocking collectives, per_device(): act = lax.all_gather(hold(act), 'z', axis=0, tiled=False)  27 us
    all_to_all x1, blocking collectives, per_device(): lax.all_to_all(partial_scores.reshape(y_n * xl_n * z_n, 1, 128), ('y', 'x...  23 us
    all_to_all x1, starting transfers between devices, per_device(): grad = lax.all_to_all(grad, 'y', 0, 0, tiled=True)  13.8 us
    ppermute x1, starting transfers between devices, per_device(): other_half = lax.ppermute(precond, 'xh', swap)  5.42 us
    all_to_all x1, starting transfers between devices, per_device(): lax.all_to_all(turned.reshape(xl_n * xh_n, 2, tokens, width), ('xl', 'xh'...  4.29 us
    ppermute x1, starting transfers between devices, per_device(): lax.ppermute(turned[:, 0], AXES, moved(lambda xl, y, c, z, xh: (xl, z, c,...  4.17 us
    pallas_call x1, Pallas kernels, rotate(): pl.pallas_call(rotate_kernel, out_shape=jax.ShapeDtypeStruct((layers, 2,...  2.33 us
    pallas_call x1, Pallas kernels, score(): pl.pallas_call(score_kernel, out_shape=jax.ShapeDtypeStruct((y_n, xl_n, 8...  2.04 us
  transfers between devices with their start and end apart: 6, of which 0 were waited for; matrix products, arithmetic and copies ran while one was open for 1% of the time, Pallas kernels for 0%

profile of v7, /device:TPU:8, one launch (start us, length us, event | category | flops | bytes accessed | tf_op | source)
XLA Modules:
  0.0 89.2 jit_solution(6640057428980239722)
XLA Ops:
  0.0 0.0 copy-start
  0.0 2.3 %shard_map.64 = bf16[2,2,2,32,320]{4,3,2,1,0:T(8,128)(2,1)} custom-call(bf16[2,64,320]{2,1,0:T(8,128)(2,1)} %bitcast.26, bf16[2,64,320]{2,1,0:T(8,128)(2,1)} %bitcast.27, bf16[2,320,320]{2,1,0:T(8,128)(2,1)} %bitcast.24, bf16[2,320,320]{2,1,0:T(8,128)(2,1)} %bitcast.25), custom_call_target="tpu_custom_call" | custom-call | flops 52428800 | bytes 2097152 | tf_op jit(solution)/shard_map/pallas_call | solution.py:51
  2.3 4.3 %all-to-all-start = ((bf16[4,2,32,320]{3,2,1,0:T(8,128)(2,1)}), bf16[4,2,32,320]{3,2,1,0:T(8,128)(2,1)S(1)}, u32[]{:S(2)}, u32[]{:S(2)}) async-start(bf16[4,2,32,320]{3,2,1,0:T(8,128)(2,1)} %bitcast.23), calls=%async_computation | async-start | bytes 393216 | tf_op jit(solution)/shard_map/all_to_all | solution.py:143
  6.6 0.0 copy-done
  6.6 5.4 %collective-permute-start.1 = (bf16[2,320,320]{2,1,0:T(8,128)(2,1)S(1)}, bf16[2,320,320]{2,1,0:T(8,128)(2,1)S(1)}, u32[]{:S(2)}, u32[]{:S(2)}) collective-permute-start(bf16[2,320,320]{2,1,0:T(8,128)(2,1)S(1)} %copy-done), channel_id=1, source_target_pairs={{0,1},{1,0},{2,3},{3,2},{4,5},{5,4},{6,7},{7,6},{8,9},{9,8},{10,11... | collective-permute-start | bytes 1228808 | tf_op jit(solution)/shard_map/ppermute | solution.py:140
  12.1 1.9 %collective-permute-start.2 = (bf16[2,320,320]{2,1,0:T(8,128)(2,1)S(1)}, bf16[2,320,320]{2,1,0:T(8,128)(2,1)S(1)}, u32[]{:S(2)}, u32[]{:S(2)}) collective-permute-start(bf16[2,320,320]{2,1,0:T(8,128)(2,1)S(1)} %copy-done), channel_id=1, source_target_pairs={{0,16},{16,0},{1,17},{17,1},{2,18},{18,2},{3,19},{19,3},{4,20},{20... | collective-permute-start | bytes 1228808 | tf_op jit(solution)/shard_map/ppermute | solution.py:152
  14.0 0.0 all-to-all-done
  14.0 4.2 %collective-permute-start = (bf16[4,32,320]{2,1,0:T(8,128)(2,1)S(1)}, bf16[4,32,320]{2,1,0:T(8,128)(2,1)S(1)}, u32[]{:S(2)}, u32[]{:S(2)}) collective-permute-start(bf16[4,32,320]{2,1,0:T(8,128)(2,1)S(1)} %get-tuple-element.6), channel_id=1, source_target_pairs={{0,0},{1,1},{2,32},{3,33},{4,64},{5,65},{6,96},{7,97},{8,128},{9,1... | collective-permute-start | bytes 245768 | tf_op jit(solution)/shard_map/ppermute | solution.py:146
  18.2 0.0 copy-start.2
  18.2 0.6 copy-done.2
  18.9 0.1 pad_add_fusion.place_ref
  18.9 1.0 %broadcast_in_dim.3 = bf16[8,4,32,320]{3,2,1,0:T(8,128)(2,1)} broadcast(bf16[4,32,320]{2,1,0:T(8,128)(2,1)S(1)} %get-tuple-element.5), dimensions={1,2,3} | broadcast | bytes 737280 | tf_op jit(solution)/shard_map/broadcast_in_dim | solution.py:147
  19.9 13.8 %all-to-all-start.1 = ((bf16[8,4,32,320]{3,2,1,0:T(8,128)(2,1)}), bf16[8,4,32,320]{3,2,1,0:T(8,128)(2,1)S(1)}, u32[]{:S(2)}, u32[]{:S(2)}) async-start(bf16[8,4,32,320]{3,2,1,0:T(8,128)(2,1)} %broadcast_in_dim.3), calls=%async_computation.1 | async-start | bytes 1572864 | tf_op jit(solution)/shard_map/all_to_all | solution.py:148
  33.8 0.0 collective-permute-done.1.tables_and_out_1_
  33.8 1.9 %collective-permute-start.3 = (bf16[2,320,320]{2,1,0:T(8,128)(2,1)S(1)}, bf16[2,320,320]{2,1,0:T(8,128)(2,1)S(1)}, u32[]{:S(2)}, u32[]{:S(2)}) collective-permute-start(bf16[2,320,320]{2,1,0:T(8,128)(2,1)S(1)} %collective-permute-done.1.tables_and_out_1_), channel_id=1, source_target_pairs={{0,16},{16,0},{1,17},{17,1},{2,18},{18,2},{3,19},{19,3},{4,20},{20... | collective-permute-start | bytes 1228808 | tf_op jit(solution)/shard_map/ppermute | solution.py:152
  35.7 0.0 collective-permute-done.rows_ref
  35.7 0.0 copy-start.1
  35.7 0.6 copy-done.1
  36.3 27.0 %all-gather = bf16[32,32,320]{2,1,0:T(8,128)(2,1)S(1)} all-gather(bf16[4,32,320]{2,1,0:T(8,128)(2,1)} %shard_map.65), channel_id=2, replica_groups=mesh['xl'=2,'y'=8,'c'=2,'z'=8,'xh'=2] {'z'}, dimensions={0}, use_global_device_ids=true | all-gather | bytes 737280 | tf_op jit(solution)/shard_map/all_gather | solution.py:149
  63.3 0.0 collective-permute-done.2.tables_and_out_2_
  63.3 0.0 collective-permute-done.3.tables_and_out_3_
  63.3 0.0 all-to-all-done.1
  63.4 2.0 %shard_map.66 = f32[8,2,8,128]{3,2,1,0:T(8,128)S(1)} custom-call(s32[6]{0:T(128)S(1)} %pad_add_fusion.place_ref, bf16[8,2,2,32,320]{4,3,2,1,0:T(8,128)(2,1)S(1)} %bitcast.21, bf16[8,2,2,32,320]{4,3,2,1,0:T(8,128)(2,1)S(1)} %bitcast.20, bf16[2,320,320]{2,1,0:T(8,128)(2,1)S(1)} %copy-done, bf16[2,320,320]{2,1,0:T(8,128)(2,1)S(1)} %collective-permute-done.1.tables_and_out_1_, ...), custom_call_target="tpu_custom_call" | custom-call | flops 838860800 | bytes 4194304 | tf_op jit(solution)/shard_map/pallas_call | solution.py:118
  65.4 23.0 %all_to_all.15 = f32[128,1,128]{2,1,0:T(1,128)S(1)} all-to-all(f32[128,1,128]{2,1,0:T(1,128)S(1)} %bitcast.22), channel_id=1, replica_groups=mesh['xl'=2,'y'=8,'c'=2,'z'=8,'xh'=2] {'y','xl','z'}, dimensions={0} | all-to-all | bytes 131072 | tf_op jit(solution)/shard_map/all_to_all | solution.py:155
  88.4 0.2 reduce_sum.9
  88.6 0.6 reshape.43
  (2 shorter events, 0.0 us)
Async XLA Ops:
  0.0 6.6 %copy-start = (bf16[2,320,320]{2,1,0:T(8,128)(2,1)S(1)}, bf16[2,320,320]{2,1,0:T(8,128)(2,1)}, u32[]{:S(2)}) copy-start(bf16[2,320,320]{2,1,0:T(8,128)(2,1)} %tables_and_out_0_.1) | copy-start | bytes 1228804
  2.3 11.7 %all-to-all-start = ((bf16[4,2,32,320]{3,2,1,0:T(8,128)(2,1)}), bf16[4,2,32,320]{3,2,1,0:T(8,128)(2,1)S(1)}, u32[]{:S(2)}, u32[]{:S(2)}) async-start(bf16[4,2,32,320]{3,2,1,0:T(8,128)(2,1)} %bitcast.23), calls=%async_computation | async-start | bytes 393216 | tf_op jit(solution)/shard_map/all_to_all | solution.py:143
  6.6 27.1 %collective-permute-start.1 = (bf16[2,320,320]{2,1,0:T(8,128)(2,1)S(1)}, bf16[2,320,320]{2,1,0:T(8,128)(2,1)S(1)}, u32[]{:S(2)}, u32[]{:S(2)}) collective-permute-start(bf16[2,320,320]{2,1,0:T(8,128)(2,1)S(1)} %copy-done), channel_id=1, source_target_pairs={{0,1},{1,0},{2,3},{3,2},{4,5},{5,4},{6,7},{7,6},{8,9},{9,8},{10,11... | collective-permute-start | bytes 1228808 | tf_op jit(solution)/shard_map/ppermute | solution.py:140
  12.1 51.3 %collective-permute-start.2 = (bf16[2,320,320]{2,1,0:T(8,128)(2,1)S(1)}, bf16[2,320,320]{2,1,0:T(8,128)(2,1)S(1)}, u32[]{:S(2)}, u32[]{:S(2)}) collective-permute-start(bf16[2,320,320]{2,1,0:T(8,128)(2,1)S(1)} %copy-done), channel_id=1, source_target_pairs={{0,16},{16,0},{1,17},{17,1},{2,18},{18,2},{3,19},{19,3},{4,20},{20... | collective-permute-start | bytes 1228808 | tf_op jit(solution)/shard_map/ppermute | solution.py:152
  14.0 21.6 %collective-permute-start = (bf16[4,32,320]{2,1,0:T(8,128)(2,1)S(1)}, bf16[4,32,320]{2,1,0:T(8,128)(2,1)S(1)}, u32[]{:S(2)}, u32[]{:S(2)}) collective-permute-start(bf16[4,32,320]{2,1,0:T(8,128)(2,1)S(1)} %get-tuple-element.6), channel_id=1, source_target_pairs={{0,0},{1,1},{2,32},{3,33},{4,64},{5,65},{6,96},{7,97},{8,128},{9,1... | collective-permute-start | bytes 245768 | tf_op jit(solution)/shard_map/ppermute | solution.py:146
  18.2 0.7 copy-start.2
  19.9 43.4 %all-to-all-start.1 = ((bf16[8,4,32,320]{3,2,1,0:T(8,128)(2,1)}), bf16[8,4,32,320]{3,2,1,0:T(8,128)(2,1)S(1)}, u32[]{:S(2)}, u32[]{:S(2)}) async-start(bf16[8,4,32,320]{3,2,1,0:T(8,128)(2,1)} %broadcast_in_dim.3), calls=%async_computation.1 | async-start | bytes 1572864 | tf_op jit(solution)/shard_map/all_to_all | solution.py:148
  33.8 29.6 %collective-permute-start.3 = (bf16[2,320,320]{2,1,0:T(8,128)(2,1)S(1)}, bf16[2,320,320]{2,1,0:T(8,128)(2,1)S(1)}, u32[]{:S(2)}, u32[]{:S(2)}) collective-permute-start(bf16[2,320,320]{2,1,0:T(8,128)(2,1)S(1)} %collective-permute-done.1.tables_and_out_1_), channel_id=1, source_target_pairs={{0,16},{16,0},{1,17},{17,1},{2,18},{18,2},{3,19},{19,3},{4,20},{20... | collective-permute-start | bytes 1228808 | tf_op jit(solution)/shard_map/ppermute | solution.py:152
  35.7 0.7 copy-start.1

commit v8 on v7

--- a/solution.py
+++ b/solution.py
@@ -51,7 +51,13 @@
     return pl.pallas_call(
         rotate_kernel,
         out_shape=jax.ShapeDtypeStruct((layers, 2, 2, tokens // 2, width), jnp.bfloat16),
-        scratch_shapes=[pltpu.VMEM((layers, 2, pl.cdiv(width, 128), tokens, 128), jnp.float32)],
+        grid=(layers,),
+        in_specs=[pl.BlockSpec((1, tokens, width), lambda layer: (layer, 0, 0))] * 2
+        + [pl.BlockSpec((1, width, width), lambda layer: (layer, 0, 0))] * 2,
+        out_specs=pl.BlockSpec(
+            (1, 2, 2, tokens // 2, width), lambda layer: (layer, 0, 0, 0, 0)
+        ),
+        scratch_shapes=[pltpu.VMEM((1, 2, pl.cdiv(width, 128), tokens, 128), jnp.float32)],
         cost_estimate=pl.CostEstimate(
             flops=4 * layers * tokens * width * width, bytes_accessed=2 << 20, transcendentals=0
         ),

time: 89.6 us -> 89.6 us (level)
  no operation moved by 1% of the time
where the time goes in v8:
time: 89.6 us; the launch traced here: 89.2 us
  blocking collectives  50 us (56%)
  starting transfers between devices  31.6 us (35%)
  Pallas kernels  4.35 us (5%)
  local copies, waits for them, and re-layouts  2.94 us (3%)
    all_gather x1, blocking collectives, per_device(): act = lax.all_gather(hold(act), 'z', axis=0, tiled=False)  27 us
    all_to_all x1, blocking collectives, per_device(): lax.all_to_all(partial_scores.reshape(y_n * xl_n * z_n, 1, 128), ('y', 'x...  23 us
    all_to_all x1, starting transfers between devices, per_device(): grad = lax.all_to_all(grad, 'y', 0, 0, tiled=True)  13.8 us
    ppermute x1, starting transfers between devices, per_device(): other_half = lax.ppermute(precond, 'xh', swap)  5.42 us
    all_to_all x1, starting transfers between devices, per_device(): lax.all_to_all(turned.reshape(xl_n * xh_n, 2, tokens, width), ('xl', 'xh'...  4.29 us
    ppermute x1, starting transfers between devices, per_device(): lax.ppermute(turned[:, 0], AXES, moved(lambda xl, y, c, z, xh: (xl, z, c,...  4.17 us
    pallas_call x1, Pallas kernels, rotate(): pl.pallas_call(rotate_kernel, out_shape=jax.ShapeDtypeStruct((layers, 2,...  2.31 us
    pallas_call x1, Pallas kernels, score(): pl.pallas_call(score_kernel, out_shape=jax.ShapeDtypeStruct((y_n, xl_n, 8...  2.04 us
  transfers between devices with their start and end apart: 6, of which 0 were waited for; matrix products, arithmetic and copies ran while one was open for 1% of the time, Pallas kernels for 0%

profile of v8, /device:TPU:8, one launch (start us, length us, event | category | flops | bytes accessed | tf_op | source)
XLA Modules:
  0.0 89.2 jit_solution(7959314387108393694)
XLA Ops:
  0.0 0.0 copy-start
  0.0 2.3 %shard_map.64 = bf16[2,2,2,32,320]{4,3,2,1,0:T(8,128)(2,1)} custom-call(bf16[2,64,320]{2,1,0:T(8,128)(2,1)} %bitcast.26, bf16[2,64,320]{2,1,0:T(8,128)(2,1)} %bitcast.27, bf16[2,320,320]{2,1,0:T(8,128)(2,1)} %bitcast.24, bf16[2,320,320]{2,1,0:T(8,128)(2,1)} %bitcast.25), custom_call_target="tpu_custom_call" | custom-call | flops 52428800 | bytes 2097152 | tf_op jit(solution)/shard_map/pallas_call | solution.py:51
  2.3 4.3 %all-to-all-start = ((bf16[4,2,32,320]{3,2,1,0:T(8,128)(2,1)}), bf16[4,2,32,320]{3,2,1,0:T(8,128)(2,1)S(1)}, u32[]{:S(2)}, u32[]{:S(2)}) async-start(bf16[4,2,32,320]{3,2,1,0:T(8,128)(2,1)} %bitcast.23), calls=%async_computation | async-start | bytes 393216 | tf_op jit(solution)/shard_map/all_to_all | solution.py:149
  6.6 0.0 copy-done
  6.6 5.4 %collective-permute-start.1 = (bf16[2,320,320]{2,1,0:T(8,128)(2,1)S(1)}, bf16[2,320,320]{2,1,0:T(8,128)(2,1)S(1)}, u32[]{:S(2)}, u32[]{:S(2)}) collective-permute-start(bf16[2,320,320]{2,1,0:T(8,128)(2,1)S(1)} %copy-done), channel_id=1, source_target_pairs={{0,1},{1,0},{2,3},{3,2},{4,5},{5,4},{6,7},{7,6},{8,9},{9,8},{10,11... | collective-permute-start | bytes 1228808 | tf_op jit(solution)/shard_map/ppermute | solution.py:146
  12.0 1.9 %collective-permute-start.2 = (bf16[2,320,320]{2,1,0:T(8,128)(2,1)S(1)}, bf16[2,320,320]{2,1,0:T(8,128)(2,1)S(1)}, u32[]{:S(2)}, u32[]{:S(2)}) collective-permute-start(bf16[2,320,320]{2,1,0:T(8,128)(2,1)S(1)} %copy-done), channel_id=1, source_target_pairs={{0,16},{16,0},{1,17},{17,1},{2,18},{18,2},{3,19},{19,3},{4,20},{20... | collective-permute-start | bytes 1228808 | tf_op jit(solution)/shard_map/ppermute | solution.py:158
  14.0 0.0 all-to-all-done
  14.0 4.2 %collective-permute-start = (bf16[4,32,320]{2,1,0:T(8,128)(2,1)S(1)}, bf16[4,32,320]{2,1,0:T(8,128)(2,1)S(1)}, u32[]{:S(2)}, u32[]{:S(2)}) collective-permute-start(bf16[4,32,320]{2,1,0:T(8,128)(2,1)S(1)} %get-tuple-element.6), channel_id=1, source_target_pairs={{0,0},{1,1},{2,32},{3,33},{4,64},{5,65},{6,96},{7,97},{8,128},{9,1... | collective-permute-start | bytes 245768 | tf_op jit(solution)/shard_map/ppermute | solution.py:152
  18.2 0.0 copy-start.2
  18.2 0.6 copy-done.2
  18.8 0.1 pad_add_fusion.place_ref
  18.9 1.0 %broadcast_in_dim.3 = bf16[8,4,32,320]{3,2,1,0:T(8,128)(2,1)} broadcast(bf16[4,32,320]{2,1,0:T(8,128)(2,1)S(1)} %get-tuple-element.5), dimensions={1,2,3} | broadcast | bytes 737280 | tf_op jit(solution)/shard_map/broadcast_in_dim | solution.py:153
  19.9 13.8 %all-to-all-start.1 = ((bf16[8,4,32,320]{3,2,1,0:T(8,128)(2,1)}), bf16[8,4,32,320]{3,2,1,0:T(8,128)(2,1)S(1)}, u32[]{:S(2)}, u32[]{:S(2)}) async-start(bf16[8,4,32,320]{3,2,1,0:T(8,128)(2,1)} %broadcast_in_dim.3), calls=%async_computation.1 | async-start | bytes 1572864 | tf_op jit(solution)/shard_map/all_to_all | solution.py:154
  33.7 0.0 collective-permute-done.1.tables_and_out_1_
  33.7 1.9 %collective-permute-start.3 = (bf16[2,320,320]{2,1,0:T(8,128)(2,1)S(1)}, bf16[2,320,320]{2,1,0:T(8,128)(2,1)S(1)}, u32[]{:S(2)}, u32[]{:S(2)}) collective-permute-start(bf16[2,320,320]{2,1,0:T(8,128)(2,1)S(1)} %collective-permute-done.1.tables_and_out_1_), channel_id=1, source_target_pairs={{0,16},{16,0},{1,17},{17,1},{2,18},{18,2},{3,19},{19,3},{4,20},{20... | collective-permute-start | bytes 1228808 | tf_op jit(solution)/shard_map/ppermute | solution.py:158
  35.7 0.0 collective-permute-done.rows_ref
  35.7 0.0 copy-start.1
  35.7 0.6 copy-done.1
  36.3 27.0 %all-gather = bf16[32,32,320]{2,1,0:T(8,128)(2,1)S(1)} all-gather(bf16[4,32,320]{2,1,0:T(8,128)(2,1)} %shard_map.65), channel_id=2, replica_groups=mesh['xl'=2,'y'=8,'c'=2,'z'=8,'xh'=2] {'z'}, dimensions={0}, use_global_device_ids=true | all-gather | bytes 737280 | tf_op jit(solution)/shard_map/all_gather | solution.py:155
  63.3 0.0 collective-permute-done.2.tables_and_out_2_
  63.3 0.0 collective-permute-done.3.tables_and_out_3_
  63.3 0.0 all-to-all-done.1
  63.3 2.0 %shard_map.66 = f32[8,2,8,128]{3,2,1,0:T(8,128)S(1)} custom-call(s32[6]{0:T(128)S(1)} %pad_add_fusion.place_ref, bf16[8,2,2,32,320]{4,3,2,1,0:T(8,128)(2,1)S(1)} %bitcast.21, bf16[8,2,2,32,320]{4,3,2,1,0:T(8,128)(2,1)S(1)} %bitcast.20, bf16[2,320,320]{2,1,0:T(8,128)(2,1)S(1)} %copy-done, bf16[2,320,320]{2,1,0:T(8,128)(2,1)S(1)} %collective-permute-done.1.tables_and_out_1_, ...), custom_call_target="tpu_custom_call" | custom-call | flops 838860800 | bytes 4194304 | tf_op jit(solution)/shard_map/pallas_call | solution.py:124
  65.4 23.0 %all_to_all.15 = f32[128,1,128]{2,1,0:T(1,128)S(1)} all-to-all(f32[128,1,128]{2,1,0:T(1,128)S(1)} %bitcast.22), channel_id=1, replica_groups=mesh['xl'=2,'y'=8,'c'=2,'z'=8,'xh'=2] {'y','xl','z'}, dimensions={0} | all-to-all | bytes 131072 | tf_op jit(solution)/shard_map/all_to_all | solution.py:161
  88.4 0.2 reduce_sum.9
  88.5 0.6 reshape.43
  (2 shorter events, 0.0 us)
Async XLA Ops:
  0.0 6.6 %copy-start = (bf16[2,320,320]{2,1,0:T(8,128)(2,1)S(1)}, bf16[2,320,320]{2,1,0:T(8,128)(2,1)}, u32[]{:S(2)}) copy-start(bf16[2,320,320]{2,1,0:T(8,128)(2,1)} %tables_and_out_0_.1) | copy-start | bytes 1228804
  2.3 11.7 %all-to-all-start = ((bf16[4,2,32,320]{3,2,1,0:T(8,128)(2,1)}), bf16[4,2,32,320]{3,2,1,0:T(8,128)(2,1)S(1)}, u32[]{:S(2)}, u32[]{:S(2)}) async-start(bf16[4,2,32,320]{3,2,1,0:T(8,128)(2,1)} %bitcast.23), calls=%async_computation | async-start | bytes 393216 | tf_op jit(solution)/shard_map/all_to_all | solution.py:149
  6.6 27.1 %collective-permute-start.1 = (bf16[2,320,320]{2,1,0:T(8,128)(2,1)S(1)}, bf16[2,320,320]{2,1,0:T(8,128)(2,1)S(1)}, u32[]{:S(2)}, u32[]{:S(2)}) collective-permute-start(bf16[2,320,320]{2,1,0:T(8,128)(2,1)S(1)} %copy-done), channel_id=1, source_target_pairs={{0,1},{1,0},{2,3},{3,2},{4,5},{5,4},{6,7},{7,6},{8,9},{9,8},{10,11... | collective-permute-start | bytes 1228808 | tf_op jit(solution)/shard_map/ppermute | solution.py:146
  12.0 51.3 %collective-permute-start.2 = (bf16[2,320,320]{2,1,0:T(8,128)(2,1)S(1)}, bf16[2,320,320]{2,1,0:T(8,128)(2,1)S(1)}, u32[]{:S(2)}, u32[]{:S(2)}) collective-permute-start(bf16[2,320,320]{2,1,0:T(8,128)(2,1)S(1)} %copy-done), channel_id=1, source_target_pairs={{0,16},{16,0},{1,17},{17,1},{2,18},{18,2},{3,19},{19,3},{4,20},{20... | collective-permute-start | bytes 1228808 | tf_op jit(solution)/shard_map/ppermute | solution.py:158
  14.0 21.6 %collective-permute-start = (bf16[4,32,320]{2,1,0:T(8,128)(2,1)S(1)}, bf16[4,32,320]{2,1,0:T(8,128)(2,1)S(1)}, u32[]{:S(2)}, u32[]{:S(2)}) collective-permute-start(bf16[4,32,320]{2,1,0:T(8,128)(2,1)S(1)} %get-tuple-element.6), channel_id=1, source_target_pairs={{0,0},{1,1},{2,32},{3,33},{4,64},{5,65},{6,96},{7,97},{8,128},{9,1... | collective-permute-start | bytes 245768 | tf_op jit(solution)/shard_map/ppermute | solution.py:152
  18.2 0.7 copy-start.2
  19.9 43.4 %all-to-all-start.1 = ((bf16[8,4,32,320]{3,2,1,0:T(8,128)(2,1)}), bf16[8,4,32,320]{3,2,1,0:T(8,128)(2,1)S(1)}, u32[]{:S(2)}, u32[]{:S(2)}) async-start(bf16[8,4,32,320]{3,2,1,0:T(8,128)(2,1)} %broadcast_in_dim.3), calls=%async_computation.1 | async-start | bytes 1572864 | tf_op jit(solution)/shard_map/all_to_all | solution.py:154
  33.7 29.6 %collective-permute-start.3 = (bf16[2,320,320]{2,1,0:T(8,128)(2,1)S(1)}, bf16[2,320,320]{2,1,0:T(8,128)(2,1)S(1)}, u32[]{:S(2)}, u32[]{:S(2)}) collective-permute-start(bf16[2,320,320]{2,1,0:T(8,128)(2,1)S(1)} %collective-permute-done.1.tables_and_out_1_), channel_id=1, source_target_pairs={{0,16},{16,0},{1,17},{17,1},{2,18},{18,2},{3,19},{19,3},{4,20},{20... | collective-permute-start | bytes 1228808 | tf_op jit(solution)/shard_map/ppermute | solution.py:158
  35.7 0.7 copy-start.1
